TPU v7x, 512 devices: a whole 4x4x16 slice. The times are simulated.
512 devices in a mesh: clus: 128 (over z, x, core), src: 4 (over y).
Axes of the slice: x: 4, y: 4, z: 16, core: 2. Of those that a mesh axis runs over, the one named last changes fastest.
Arguments:
- embeddings: float32 [65536, 768], P(('clus', 'src'))
- cluster: int32 [65536], P(('clus', 'src')), may hold values from 0 to 1023, as said below
Outputs:
- centroids: float32 [1024, 768], P('clus')
- nearest: float32 [65536], P(('clus', 'src'))
Inputs may be any that keep to these rules, and one draw needn't show every extreme that they name: Of one device's 128 rows, at most 2 have clusters of one owner (cluster // 8); one owner receives exactly 2 rows from every device.
All inputs are finite; a program needn't handle non-finite values.
Results may differ from a plain program's by a relative error of at most 0.00032.
Values may be sent and summed in bfloat16 or wider, within the bound.
No kernel may reach another device: no remote copies, remote signals or barrier semaphores. Data moves between devices by JAX's collectives and lax.ppermute only.
A program may use at most 64 MiB of HBM per device.

v0:
```python
import jax
import jax.numpy as jnp
from jax import lax
from jax.sharding import PartitionSpec as P

CLUS_DEV = 8


def block_maxima(current, own_unit, own_labels, own_global, other_unit, other_labels, other_global):
    scores = lax.dot_general(
        own_unit, other_unit, (((1,), (1,)), ((), ())), preferred_element_type=jnp.float32
    )
    allowed = (
        (own_labels[:, None] == other_labels[None, :])
        & (own_global[:, None] != other_global[None, :])
        & (own_labels[:, None] >= 0)
    )
    return jnp.maximum(current, jnp.max(jnp.where(allowed, scores, jnp.float32(-1.0)), axis=1))


def unit_rows(values):
    return (values * lax.rsqrt(jnp.sum(values * values, axis=1, keepdims=True) + 1e-06)).astype(
        jnp.bfloat16
    )


def normalized(owned):
    return owned * lax.rsqrt(jnp.sum(owned * owned, axis=1, keepdims=True) + 1e-06)


def on_device(embeddings, cluster):
    row_count = embeddings.shape[0]
    feature_dim = embeddings.shape[1]
    clus_count = lax.axis_size("clus")
    source_count = lax.axis_size("src")
    capacity = max(2, 2 * row_count // clus_count)
    slot_total = clus_count * capacity
    owner = cluster // CLUS_DEV
    member_hits = (owner[:, None] == jnp.arange(clus_count, dtype=jnp.int32)[None, :]).astype(
        jnp.int32
    )
    running = jnp.cumsum(member_hits, axis=0)
    position = jnp.sum(member_hits * running, axis=1) - 1
    slot_index = owner * capacity + position
    device_number = lax.axis_index("clus") * source_count + lax.axis_index("src")
    global_row = device_number * row_count + jnp.arange(row_count, dtype=jnp.int32)
    send_labels = jnp.full((slot_total,), -1, jnp.int32).at[slot_index].set(cluster)
    send_global = jnp.full((slot_total,), -1, jnp.int32).at[slot_index].set(global_row)
    count = lax.axis_size("clus") * CLUS_DEV
    inside = (cluster >= 0) & (cluster < count)
    segment = jnp.where(inside, cluster, count)
    owned = lax.psum_scatter(
        jax.ops.segment_sum(embeddings, segment, num_segments=count + 1)[:count],
        "clus",
        scatter_dimension=0,
        tiled=True,
    )
    owned = lax.psum(owned, "src")
    centroids = normalized(owned)
    unit = unit_rows(embeddings)
    send_unit = jnp.zeros((slot_total, feature_dim), jnp.bfloat16).at[slot_index].set(unit)
    received, recv_labels, recv_global = (
        lax.all_to_all(send_unit, "clus", split_axis=0, concat_axis=0, tiled=True),
        lax.all_to_all(send_labels, "clus", split_axis=0, concat_axis=0, tiled=True),
        lax.all_to_all(send_global, "clus", split_axis=0, concat_axis=0, tiled=True),
    )
    initial = jnp.full((slot_total,), -1.0, jnp.float32)
    piece_unit = lax.all_gather(received, "src", axis=0, tiled=True)
    piece_labels = lax.all_gather(recv_labels, "src", axis=0, tiled=True)
    piece_global = lax.all_gather(recv_global, "src", axis=0, tiled=True)
    length = piece_unit.shape[0]
    stacked = (
        piece_unit.reshape(length // slot_total, slot_total, feature_dim),
        piece_labels.reshape(length // slot_total, slot_total),
        piece_global.reshape(length // slot_total, slot_total),
    )

    def stepper(carried, sliced):
        return (
            block_maxima(
                carried, received, recv_labels, recv_global, sliced[0], sliced[1], sliced[2]
            ),
            None,
        )

    result, unused = lax.scan(stepper, initial, stacked)
    returned = lax.all_to_all(result, "clus", split_axis=0, concat_axis=0, tiled=True)
    nearest = returned[slot_index]
    return (centroids, nearest)


def solution(mesh):
    placed = (P(("clus", "src"), None), P(("clus", "src")))
    return jax.shard_map(
        on_device,
        mesh=mesh,
        in_specs=placed,
        out_specs=(P("clus", None), P(("clus", "src"))),
        check_vma=False,
    )
```

profile of v0, /device:TPU:6, one launch (start us, length us, event | category | flops | bytes accessed | tf_op | source)
XLA Modules:
  0.0 345.2 jit_solution(9316626056068664059)
XLA Ops:
  8.0 1.1 multiply_reduce_fusion
  10.3 1.8 scatter_custom_fusion.3
  12.2 46.7 %all_to_all.48 = bf16[128,2,768]{2,1,0:T(2,128)(2,1)S(1)} all-to-all(bf16[128,2,768]{2,1,0:T(2,128)(2,1)S(1)} %all_to_all.38), channel_id=1, replica_groups=mesh['clus'=128,'src'=4] {'clus'}, dimensions={0} | all-to-all | bytes 786432 | tf_op jit(solution)/shard_map/all_to_all | solution.py:63
  58.9 0.9 all_to_all.40
  59.9 2.6 scatter_custom_fusion
  62.5 1.9 slice.6
  64.4 1.2 scatter_custom_fusion.1
  66.4 6.8 %all-to-all-start = ((s32[128,2,1]{1,2,0:T(1,128)}), s32[128,2,1]{1,2,0:T(1,128)S(1)}, u32[]{:S(2)}, u32[]{:S(2)}) async-start(s32[128,2,1]{1,2,0:T(1,128)} %bitcast), calls=%async_computation.1 | async-start | bytes 131072 | tf_op jit(solution)/shard_map/all_to_all | solution.py:64
  73.3 1.0 scatter_custom_fusion.2
  75.0 12.0 %all-to-all-done = s32[128,2,1]{1,2,0:T(1,128)S(1)} async-done(((s32[128,2,1]{1,2,0:T(1,128)}), s32[128,2,1]{1,2,0:T(1,128)S(1)}, u32[]{:S(2)}, u32[]{:S(2)}) %all-to-all-start) | async-done | bytes 1056 | tf_op jit(solution)/shard_map/all_to_all | solution.py:64
  87.0 6.8 %all-to-all-start.1 = ((s32[128,2,1]{1,2,0:T(1,128)}), s32[128,2,1]{1,2,0:T(1,128)S(1)}, u32[]{:S(2)}, u32[]{:S(2)}) async-start(s32[128,2,1]{1,2,0:T(1,128)} %bitcast.1), calls=%async_computation.2 | async-start | bytes 131072 | tf_op jit(solution)/shard_map/all_to_all | solution.py:65
  93.9 10.0 %all-gather = s32[4,1,256]{2,1,0:T(1,128)S(1)} all-gather(s32[1,1,256]{2,1,0:T(1,128)S(1)} %reshape.88), channel_id=1, replica_groups=mesh['clus'=128,'src'=4] {'src'}, dimensions={0}, use_global_device_ids=true | all-gather | bytes 5120 | tf_op jit(solution)/shard_map/all_gather | solution.py:69
  103.9 3.7 %all-to-all-done.1 = s32[128,2,1]{1,2,0:T(1,128)S(1)} async-done(((s32[128,2,1]{1,2,0:T(1,128)}), s32[128,2,1]{1,2,0:T(1,128)S(1)}, u32[]{:S(2)}, u32[]{:S(2)}) %all-to-all-start.1) | async-done | bytes 1056 | tf_op jit(solution)/shard_map/all_to_all | solution.py:65
  107.7 10.0 %all-gather.1 = s32[4,1,256]{2,1,0:T(1,128)S(1)} all-gather(s32[1,1,256]{2,1,0:T(1,128)S(1)} %reshape.90), channel_id=1, replica_groups=mesh['clus'=128,'src'=4] {'src'}, dimensions={0}, use_global_device_ids=true | all-gather | bytes 5120 | tf_op jit(solution)/shard_map/all_gather | solution.py:70
  120.2 5.6 %while.11 = (s32[]{:T(128)}, f32[256]{0:T(256)S(1)}, s32[256]{0:T(256)S(1)}, s32[4,256]{1,0:T(4,128)S(1)}, s32[256]{0:T(256)S(1)}, /*index=5*/s32[4,256]{1,0:T(4...) while((s32[]{:T(128)}, f32[256]{0:T(256)S(1)}, ...), condition=%wide.region_12.13_spmd.clone, body=%wide.region_10.12_spmd.clone.sunk | while | flops 101057024 | bytes 800383 | solution.py:86
  120.2 1.3 fusion.21
  121.6 1.3 fusion.21
  123.0 1.3 fusion.21
  124.4 1.3 fusion.21
  126.5 9.7 %all-to-all-start.3 = ((f32[128,2,1]{1,2,0:T(1,128)}), f32[128,2,1]{1,2,0:T(1,128)S(1)}, u32[]{:S(2)}, u32[]{:S(2)}) async-start(f32[128,2,1]{1,2,0:T(1,128)} %bitcast.3), calls=%async_computation.4 | async-start | bytes 131072 | tf_op jit(solution)/shard_map/all_to_all | solution.py:87
  136.2 13.7 %all-to-all-done.3 = f32[128,2,1]{1,2,0:T(1,128)S(1)} async-done(((f32[128,2,1]{1,2,0:T(1,128)}), f32[128,2,1]{1,2,0:T(1,128)S(1)}, u32[]{:S(2)}, u32[]{:S(2)}) %all-to-all-start.3) | async-done | bytes 1056 | tf_op jit(solution)/shard_map/all_to_all | solution.py:87
  151.4 1.8 gather_fusion
  153.2 166.0 %reduce-scatter.2.cloned.1.call-done = f32[8,768]{1,0:T(8,128)} async-done(((f32[1024,768]{1,0:T(8,128)}), f32[8,768]{1,0:T(8,128)}) %reduce-scatter.2.cloned.1.call-update) | async-done | bytes 24592 | tf_op jit(solution)/shard_map/reduce_scatter | solution.py:52
  319.2 17.7 %psum.7 = f32[8,768]{1,0:T(8,128)S(1)} all-reduce(f32[8,768]{1,0:T(8,128)} %reduce-scatter.2.cloned.1.call-done), channel_id=1, replica_groups=mesh['clus'=128,'src'=4] {'src'}, use_global_device_ids=true, to_apply=%region_2.3 | all-reduce | flops 6144 | bytes 49152 | tf_op jit(solution)/shard_map/psum | solution.py:58
  (47 shorter events, 8.7 us)
Async XLA Ops:
  8.0 112.2 %all-gather.4.cloned.1.call-start = ((), (), s32[]{:S(2)}) async-start(), calls=%async_computation.6 | async-start | bytes 1966080 | tf_op jit(solution)/shard_map/all_gather | solution.py:68
  59.9 259.4 %reduce-scatter.2.cloned.1.call-start = ((), (), s32[]{:S(2)}) async-start(), calls=%async_computation.5 | async-start | bytes 3170304 | tf_op jit(solution)/shard_map/reduce_scatter | solution.py:52
  64.4 55.8 %copy-start = (bf16[256,768]{1,0:T(8,128)(2,1)S(1)}, bf16[256,768]{1,0:T(8,128)(2,1)}, u32[]{:S(2)}) copy-start(bf16[256,768]{1,0:T(8,128)(2,1)} %all_to_all.40) | copy-start | bytes 1179652
  66.4 20.6 %all-to-all-start = ((s32[128,2,1]{1,2,0:T(1,128)}), s32[128,2,1]{1,2,0:T(1,128)S(1)}, u32[]{:S(2)}, u32[]{:S(2)}) async-start(s32[128,2,1]{1,2,0:T(1,128)} %bitcast), calls=%async_computation.1 | async-start | bytes 131072 | tf_op jit(solution)/shard_map/all_to_all | solution.py:64
  87.0 20.6 %all-to-all-start.1 = ((s32[128,2,1]{1,2,0:T(1,128)}), s32[128,2,1]{1,2,0:T(1,128)S(1)}, u32[]{:S(2)}, u32[]{:S(2)}) async-start(s32[128,2,1]{1,2,0:T(1,128)} %bitcast.1), calls=%async_computation.2 | async-start | bytes 131072 | tf_op jit(solution)/shard_map/all_to_all | solution.py:65
  126.5 23.5 %all-to-all-start.3 = ((f32[128,2,1]{1,2,0:T(1,128)}), f32[128,2,1]{1,2,0:T(1,128)S(1)}, u32[]{:S(2)}, u32[]{:S(2)}) async-start(f32[128,2,1]{1,2,0:T(1,128)} %bitcast.3), calls=%async_computation.4 | async-start | bytes 131072 | tf_op jit(solution)/shard_map/all_to_all | solution.py:87
Sparse Core Ops, SparseCore 0:
  60.0 26.0 all-gather.3
Sparse Core Ops, SparseCore 1:
  65.0 254.2 reduce-scatter.1
where the time goes:
time: 346 us; the launch traced here: 345 us
  waiting for transfers between devices  195 us (56%)
  blocking collectives  84.3 us (24%)
  starting transfers between devices  23.4 us (7%)
  between operations  15.7 us (5%)
  local copies, waits for them, and re-layouts  10.9 us (3%)
  other arithmetic  9.94 us (3%)
  matrix products  5.32 us (2%)
    reduce_scatter x1, waiting for transfers between devices, on_device(): lax.psum_scatter(jax.ops.segment_sum(embeddings, segment, num_segments=co...  166 us
    all_to_all x1, blocking collectives, on_device(): lax.all_to_all(send_unit, 'clus', split_axis=0, concat_axis=0, tiled=True)  46.7 us
    psum x1, blocking collectives, on_device(): owned = lax.psum(owned, 'src')  17.7 us
    all_to_all x1, waiting for transfers between devices, on_device(): lax.all_to_all(result, 'clus', split_axis=0, concat_axis=0, tiled=True)  13.7 us
    all_to_all x1, waiting for transfers between devices, on_device(): lax.all_to_all(send_labels, 'clus', split_axis=0, concat_axis=0, tiled=True)  12 us
    all_gather x1, blocking collectives, on_device(): piece_labels = lax.all_gather(recv_labels, 'src', axis=0, tiled=True)  9.98 us
    all_gather x1, blocking collectives, on_device(): piece_global = lax.all_gather(recv_global, 'src', axis=0, tiled=True)  9.98 us
    all_to_all x1, starting transfers between devices, on_device(): lax.all_to_all(result, 'clus', split_axis=0, concat_axis=0, tiled=True)  9.7 us
  transfers between devices with their start and end apart: 5, of which 4 were waited for; matrix products, arithmetic and copies ran while one was open for 5% of the time, Pallas kernels for 0%

commit v1 on v0

v1 whole, which is shorter than its diff:
```python
import jax
import jax.numpy as jnp
from jax import lax
from jax.experimental import pallas as pl
from jax.experimental.pallas import tpu as pltpu
from jax.sharding import PartitionSpec as P

CLUS_DEV = 8
OWNERS = 128
ROWS = 128
DIM = 768
WIDE = DIM + 128
EXTRA = 32
F32_EDGE = 3.38e38
VMEM = pltpu.CompilerParams(vmem_limit_bytes=48 * 1024 * 1024)


def pieces(value):
    high = jnp.clip(value, -F32_EDGE, F32_EDGE).astype(jnp.bfloat16)
    rest = value - high.astype(jnp.float32)
    middle = rest.astype(jnp.bfloat16)
    low = (rest - middle.astype(jnp.float32)).astype(jnp.bfloat16)
    return high, middle, low


def product(left, right, contract):
    return lax.dot_general(
        left, right, (contract, ((), ())), preferred_element_type=jnp.float32
    )


def place_kernel(rows_ref, cluster_ref, out_ref, code_ref):
    cluster = cluster_ref[...]
    owner = cluster // CLUS_DEV
    label = (cluster - owner * CLUS_DEV + 1).astype(jnp.float32)
    first = lax.broadcasted_iota(jnp.int32, (OWNERS, ROWS), 0)
    second = lax.broadcasted_iota(jnp.int32, (OWNERS, ROWS), 1)
    hits = first == owner
    earlier = product(
        hits.astype(jnp.bfloat16), (first < second).astype(jnp.bfloat16), ((1,), (0,))
    )
    split = pieces(rows_ref[...])
    for slot in range(2):
        chosen = jnp.where(hits & ((earlier > 0.5) == (slot == 1)), 1.0, 0.0)
        if slot == 1:
            code_ref[...] = owner * 2 + jnp.sum(chosen, axis=0, keepdims=True).astype(jnp.int32)
        mask = chosen.astype(jnp.bfloat16)
        placed = [product(mask, piece, ((1,), (0,))) for piece in split]
        out_ref[:, slot, :DIM] = (placed[0] + placed[1]) + placed[2]
        out_ref[:, slot, DIM:] = jnp.broadcast_to(
            jnp.sum(chosen * label, axis=1, keepdims=True), (OWNERS, 128)
        )


def unit_kernel(received_ref, packed_ref, label_ref):
    sums = jnp.zeros((128, DIM), jnp.float32)
    lane = lax.broadcasted_iota(jnp.int32, (OWNERS, 128), 1).astype(jnp.float32)
    weight = lax.broadcasted_iota(jnp.int32, (8, 128), 1).astype(jnp.float32) + 1.0
    rows_of_labels = []
    for slot in range(2):
        rows = received_ref[:, slot, :DIM]
        label = received_ref[:, slot, DIM:]
        here = slice(slot * OWNERS, (slot + 1) * OWNERS)
        label_ref[here, :] = label
        scale = lax.rsqrt(jnp.sum(rows * rows, axis=1, keepdims=True) + 1e-06)
        packed_ref[here, :] = (rows * scale).astype(jnp.bfloat16)
        member = (label == lane + 1.0).astype(jnp.bfloat16)
        for piece in pieces(rows):
            sums = sums + product(member, piece, ((0,), (0,)))
        rows_of_labels.append(product(weight.astype(jnp.bfloat16), member, ((1,), (1,))))
    high, middle, low = pieces(sums[:CLUS_DEV])
    packed_ref[256:272, :] = jnp.concatenate(
        [high.astype(jnp.float32), middle.astype(jnp.float32)], axis=0
    ).astype(jnp.bfloat16)
    label_rows = jnp.concatenate(rows_of_labels + [jnp.zeros((8, DIM - 256), jnp.float32)], axis=1)
    packed_ref[272:288, :] = jnp.concatenate(
        [low.astype(jnp.float32), label_rows], axis=0
    ).astype(jnp.bfloat16)


def score_kernel(label_ref, own_ref, next_ref, last_ref, across_ref, best_ref, centroid_ref):
    label = label_ref[:, :1]
    own = own_ref[:256, :]
    not_self = lax.broadcasted_iota(jnp.int32, (256, 256), 0) != lax.broadcasted_iota(
        jnp.int32, (256, 256), 1
    )
    best = jnp.full((256, 256), -1.0, jnp.float32)
    parts = []
    for ref in (own_ref, next_ref, last_ref, across_ref):
        scores = product(own, ref[:256, :], ((1,), (1,)))
        tail = ref[272:288, :].astype(jnp.float32)
        allowed = label == tail[8:9, :256]
        if ref is own_ref:
            allowed = allowed & not_self
        best = jnp.maximum(best, jnp.where(allowed, scores, -1.0))
        head = ref[256:272, :].astype(jnp.float32)
        parts.append((head[:8] + head[8:]) + tail[:8])
    most = jnp.max(best, axis=1, keepdims=True)
    lane = lax.broadcasted_iota(jnp.int32, (OWNERS, 128), 1)
    best_ref[...] = jnp.where(lane < 64, most[:128], most[128:])
    sums = (parts[0] + parts[3]) + (parts[1] + parts[2])
    centroid_ref[...] = sums * lax.rsqrt(jnp.sum(sums * sums, axis=1, keepdims=True) + 1e-06)


def pick_kernel(returned_ref, code_ref, nearest_ref):
    code = code_ref[...]
    owner = code // 2
    first_slot = code == owner * 2
    values = jnp.where(first_slot, returned_ref[:, :1], returned_ref[:, 127:])
    mine = lax.broadcasted_iota(jnp.int32, (OWNERS, ROWS), 0) == owner
    nearest_ref[...] = jnp.sum(jnp.where(mine, values, 0.0), axis=0, keepdims=True)


def call(kernel, outs, *operands):
    spec = pl.BlockSpec(memory_space=pltpu.VMEM)
    many = isinstance(outs, list)
    return pl.pallas_call(
        kernel,
        out_shape=outs,
        in_specs=[spec] * len(operands),
        out_specs=[spec] * len(outs) if many else spec,
        compiler_params=VMEM,
    )(*operands)


def on_device(embeddings, cluster):
    shape = jax.ShapeDtypeStruct
    sent, code = call(
        place_kernel,
        [shape((OWNERS, 2, WIDE), jnp.float32), shape((1, ROWS), jnp.int32)],
        embeddings,
        cluster.reshape(1, ROWS),
    )
    received = lax.all_to_all(sent, "clus", split_axis=0, concat_axis=0, tiled=True)
    packed, label = call(
        unit_kernel,
        [shape((256 + EXTRA, DIM), jnp.bfloat16), shape((256, 128), jnp.float32)],
        received,
    )
    others = [
        lax.ppermute(packed, "src", [(i, (i + step) % 4) for i in range(4)]) for step in (3, 1, 2)
    ]
    best, centroids = call(
        score_kernel,
        [shape((OWNERS, 128), jnp.float32), shape((CLUS_DEV, DIM), jnp.float32)],
        label,
        packed,
        *others,
    )
    returned = lax.all_to_all(best, "clus", split_axis=0, concat_axis=0, tiled=True)
    nearest = call(pick_kernel, shape((1, ROWS), jnp.float32), returned, code)
    return centroids, nearest.reshape(ROWS)


def solution(mesh):
    return jax.shard_map(
        on_device,
        mesh=mesh,
        in_specs=(P(("clus", "src"), None), P(("clus", "src"))),
        out_specs=(P("clus", None), P(("clus", "src"))),
        check_vma=False,
    )
```

time: 346 us -> 127 us (0.37)
  the two profiles are of different devices: /device:TPU:6 before, /device:TPU:1 now
where the time goes in v1:
time: 127 us
  blocking collectives  92.2 us (73%)
  waiting for transfers between devices  13.2 us (10%)
  starting transfers between devices  11.3 us (9%)
  Pallas kernels  7.55 us (6%)
  local copies, waits for them, and re-layouts  1.64 us (1%)
    all_to_all x1, blocking collectives, on_device(): lax.all_to_all(sent, 'clus', split_axis=0, concat_axis=0, tiled=True)  66.7 us
    all_to_all x1, blocking collectives, on_device(): lax.all_to_all(best, 'clus', split_axis=0, concat_axis=0, tiled=True)  25.5 us
    ppermute x3, waiting for transfers between devices, on_device(): lax.ppermute(packed, 'src', [(i, (i + step) % 4) for i in range(4)])  13.2 us
    ppermute x3, starting transfers between devices, on_device(): lax.ppermute(packed, 'src', [(i, (i + step) % 4) for i in range(4)])  11.3 us
    pallas_call x4, Pallas kernels, call(): pl.pallas_call(kernel, out_shape=outs, in_specs=[spec] * len(operands), o...  7.55 us
  transfers between devices with their start and end apart: 3, of which 2 were waited for; matrix products, arithmetic and copies ran while one was open for 0% of the time, Pallas kernels for 0%

profile of v1, /device:TPU:1, one launch (start us, length us, event | category | flops | bytes accessed | tf_op | source)
XLA Modules:
  0.0 126.6 jit_solution(14601908644066956888)
XLA Ops:
  0.6 0.0 copy-start.1
  0.6 0.6 copy-done.1
  1.3 0.0 copy-start
  1.3 1.0 copy-done
  2.3 0.7 shard_map.41
  3.0 66.7 %all_to_all.16.received_ref = f32[128,2,896]{2,1,0:T(2,128)S(1)} all-to-all(f32[128,2,896]{2,1,0:T(2,128)S(1)} %get-tuple-element.8), channel_id=1, replica_groups=mesh['clus'=128,'src'=4] {'clus'}, dimensions={0} | all-to-all | bytes 1835008 | tf_op jit(solution)/shard_map/all_to_all | solution.py:134
  69.6 5.0 %shard_map.42 = (bf16[288,768]{1,0:T(8,128)(2,1)S(1)}, f32[256,128]{1,0:T(8,128)S(1)}) custom-call(f32[128,2,896]{2,1,0:T(2,128)S(1)} %all_to_all.16.received_ref), custom_call_target="tpu_custom_call" | custom-call | tf_op jit(solution)/shard_map/pallas_call | solution.py:117
  74.7 4.8 %collective-permute-start.2 = (bf16[288,768]{1,0:T(8,128)(2,1)S(1)}, bf16[288,768]{1,0:T(8,128)(2,1)S(1)}, u32[]{:S(2)}, u32[]{:S(2)}) collective-permute-start(bf16[288,768]{1,0:T(8,128)(2,1)S(1)} %get-tuple-element.10.own_ref), channel_id=1, source_target_pairs={{0,2},{1,3},{2,0},{3,1},{4,6},{5,7},{6,4},{7,5},{8,10},{9,11},{10,... | collective-permute-start | bytes 1327112 | tf_op jit(solution)/shard_map/ppermute | solution.py:141
  79.5 2.3 %collective-permute-start.1 = (bf16[288,768]{1,0:T(8,128)(2,1)S(1)}, bf16[288,768]{1,0:T(8,128)(2,1)S(1)}, u32[]{:S(2)}, u32[]{:S(2)}) collective-permute-start(bf16[288,768]{1,0:T(8,128)(2,1)S(1)} %get-tuple-element.10.own_ref), channel_id=1, source_target_pairs={{0,1},{1,2},{2,3},{3,0},{4,5},{5,6},{6,7},{7,4},{8,9},{9,10},{10,1... | collective-permute-start | bytes 1327112 | tf_op jit(solution)/shard_map/ppermute | solution.py:141
  81.8 4.2 %collective-permute-start = (bf16[288,768]{1,0:T(8,128)(2,1)S(1)}, bf16[288,768]{1,0:T(8,128)(2,1)S(1)}, u32[]{:S(2)}, u32[]{:S(2)}) collective-permute-start(bf16[288,768]{1,0:T(8,128)(2,1)S(1)} %get-tuple-element.10.own_ref), channel_id=1, source_target_pairs={{0,3},{1,0},{2,1},{3,2},{4,7},{5,4},{6,5},{7,6},{8,11},{9,8},{10,9... | collective-permute-start | bytes 1327112 | tf_op jit(solution)/shard_map/ppermute | solution.py:141
  86.0 1.5 %collective-permute-done.2.across_ref = bf16[288,768]{1,0:T(8,128)(2,1)S(1)} collective-permute-done((bf16[288,768]{1,0:T(8,128)(2,1)S(1)}, bf16[288,768]{1,0:T(8,128)(2,1)S(1)}, u32[]{:S(2)}, u32[]{:S(2)}) %collective-permute-start.2) | collective-permute-done | bytes 442400 | tf_op jit(solution)/shard_map/ppermute | solution.py:141
  87.5 11.7 %collective-permute-done.1.last_ref = bf16[288,768]{1,0:T(8,128)(2,1)S(1)} collective-permute-done((bf16[288,768]{1,0:T(8,128)(2,1)S(1)}, bf16[288,768]{1,0:T(8,128)(2,1)S(1)}, u32[]{:S(2)}, u32[]{:S(2)}) %collective-permute-start.1) | collective-permute-done | bytes 442400 | tf_op jit(solution)/shard_map/ppermute | solution.py:141
  99.2 0.0 collective-permute-done.next_ref
  99.2 1.2 shard_map.43
  100.4 25.5 %all_to_all.17 = f32[128,1,128]{2,1,0:T(1,128)S(1)} all-to-all(f32[128,1,128]{2,1,0:T(1,128)S(1)} %bitcast.7), channel_id=1, replica_groups=mesh['clus'=128,'src'=4] {'clus'}, dimensions={0} | all-to-all | bytes 131072 | tf_op jit(solution)/shard_map/all_to_all | solution.py:150
  126.0 0.6 shard_map.44
Async XLA Ops:
  0.6 0.7 copy-start.1
  1.3 1.0 copy-start
  74.7 12.8 %collective-permute-start.2 = (bf16[288,768]{1,0:T(8,128)(2,1)S(1)}, bf16[288,768]{1,0:T(8,128)(2,1)S(1)}, u32[]{:S(2)}, u32[]{:S(2)}) collective-permute-start(bf16[288,768]{1,0:T(8,128)(2,1)S(1)} %get-tuple-element.10.own_ref), channel_id=1, source_target_pairs={{0,2},{1,3},{2,0},{3,1},{4,6},{5,7},{6,4},{7,5},{8,10},{9,11},{10,... | collective-permute-start | bytes 1327112 | tf_op jit(solution)/shard_map/ppermute | solution.py:141
  79.5 19.7 %collective-permute-start.1 = (bf16[288,768]{1,0:T(8,128)(2,1)S(1)}, bf16[288,768]{1,0:T(8,128)(2,1)S(1)}, u32[]{:S(2)}, u32[]{:S(2)}) collective-permute-start(bf16[288,768]{1,0:T(8,128)(2,1)S(1)} %get-tuple-element.10.own_ref), channel_id=1, source_target_pairs={{0,1},{1,2},{2,3},{3,0},{4,5},{5,6},{6,7},{7,4},{8,9},{9,10},{10,1... | collective-permute-start | bytes 1327112 | tf_op jit(solution)/shard_map/ppermute | solution.py:141
  81.8 17.4 %collective-permute-start = (bf16[288,768]{1,0:T(8,128)(2,1)S(1)}, bf16[288,768]{1,0:T(8,128)(2,1)S(1)}, u32[]{:S(2)}, u32[]{:S(2)}) collective-permute-start(bf16[288,768]{1,0:T(8,128)(2,1)S(1)} %get-tuple-element.10.own_ref), channel_id=1, source_target_pairs={{0,3},{1,0},{2,1},{3,2},{4,7},{5,4},{6,5},{7,6},{8,11},{9,8},{10,9... | collective-permute-start | bytes 1327112 | tf_op jit(solution)/shard_map/ppermute | solution.py:141

commit v2 on v1

v2 whole, which is shorter than its diff:
```python
import jax
import jax.numpy as jnp
from jax import lax
from jax.experimental import pallas as pl
from jax.experimental.pallas import tpu as pltpu
from jax.sharding import PartitionSpec as P

CLUS_DEV = 8
OWNERS = 128
ROWS = 128
SLOTS = 256
DIM = 768
WIDE = DIM + 128
EDGE = 3.38e38
VMEM = pltpu.CompilerParams(vmem_limit_bytes=48 * 1024 * 1024)


def narrow(value):
    return jnp.clip(value, -EDGE, EDGE).astype(jnp.bfloat16)


def pieces(value):
    high = narrow(value)
    rest = value - high.astype(jnp.float32)
    middle = rest.astype(jnp.bfloat16)
    low = (rest - middle.astype(jnp.float32)).astype(jnp.bfloat16)
    return high, middle, low


def product(left, right, contract):
    return lax.dot_general(
        left, right, (contract, ((), ())), preferred_element_type=jnp.float32
    )


def iota(shape, dimension):
    return lax.broadcasted_iota(jnp.int32, shape, dimension)


def place_kernel(rows_ref, cluster_ref, unit_ref, rest_ref, code_ref):
    cluster = cluster_ref[...]
    owner = cluster // CLUS_DEV
    label = cluster - owner * CLUS_DEV
    first = iota((OWNERS, ROWS), 0)
    second = iota((OWNERS, ROWS), 1)
    hits = first == owner
    earlier = product(
        hits.astype(jnp.bfloat16), (first < second).astype(jnp.bfloat16), ((1,), (0,))
    )
    position = jnp.sum(jnp.where(hits & (earlier > 0.5), 1, 0), axis=0, keepdims=True)
    code = owner * 2 + position
    code_ref[...] = code
    chosen = (iota((SLOTS, ROWS), 0) == code).astype(jnp.bfloat16)

    rows = rows_ref[...]
    square = jnp.sum(rows * rows, axis=1, keepdims=True) + 1e-06
    scale = lax.rsqrt(square)
    norm = jnp.where(square < EDGE, square * scale, 0.0)
    unit = (rows * scale).astype(jnp.bfloat16)
    rest = narrow(rows - norm * unit.astype(jnp.float32))
    unit_ref[:, :DIM] = product(chosen, unit, ((1,), (0,))).astype(jnp.bfloat16)
    rest_ref[...] = product(chosen, rest, ((1,), (0,))).astype(jnp.bfloat16)

    high, middle, low = pieces(norm)
    norms = jnp.where(
        second == 8,
        high.astype(jnp.float32),
        jnp.where(
            second == 9,
            middle.astype(jnp.float32),
            jnp.where(second == 10, low.astype(jnp.float32), 0.0),
        ),
    ).astype(jnp.bfloat16)
    labels = (first == label).astype(jnp.bfloat16)
    unit_ref[:, DIM:] = (
        product(chosen, norms, ((1,), (0,))) + product(chosen, labels, ((1,), (1,)))
    ).astype(jnp.bfloat16)


def member_of(ref):
    tail = ref[:, DIM:]
    return jnp.where(iota((SLOTS, 128), 1) < CLUS_DEV, tail, jnp.zeros_like(tail))


def score_kernel(own_ref, next_ref, last_ref, across_ref, best_ref):
    own = own_ref[:, :DIM]
    own_member = member_of(own_ref)
    not_self = iota((SLOTS, SLOTS), 0) != iota((SLOTS, SLOTS), 1)
    best = jnp.full((SLOTS, SLOTS), -1.0, jnp.float32)
    for ref in (own_ref, next_ref, last_ref, across_ref):
        scores = product(own, ref[:, :DIM], ((1,), (1,)))
        allowed = product(own_member, member_of(ref), ((1,), (1,))) > 0.5
        if ref is own_ref:
            allowed = allowed & not_self
        best = jnp.maximum(best, jnp.where(allowed, scores, -1.0))
    most = jnp.max(best, axis=1, keepdims=True)
    slot, lane = iota((SLOTS, 128), 0), iota((SLOTS, 128), 1)
    spread = jnp.where((lane < 64) == (slot % 2 == 0), most, 0.0)
    pair = (iota((OWNERS, SLOTS), 1) // 2 == iota((OWNERS, SLOTS), 0)).astype(jnp.bfloat16)
    high, middle, low = [product(pair, piece, ((1,), (0,))) for piece in pieces(spread)]
    best_ref[...] = (high + middle) + low


def sum_kernel(unit_ref, rest_ref, sum_ref):
    tail = unit_ref[:, DIM:].astype(jnp.float32)
    norm = (tail[:, 8:9] + tail[:, 9:10]) + tail[:, 10:11]
    member = member_of(unit_ref)
    sums = product(member, rest_ref[...], ((0,), (0,)))
    for piece in pieces(member.astype(jnp.float32) * norm):
        sums = sums + product(piece, unit_ref[:, :DIM], ((0,), (0,)))
    sum_ref[...] = sums[:CLUS_DEV]


def centroid_kernel(parts_ref, centroid_ref):
    sums = (parts_ref[:8] + parts_ref[8:16]) + (parts_ref[16:24] + parts_ref[24:])
    centroid_ref[...] = sums * lax.rsqrt(jnp.sum(sums * sums, axis=1, keepdims=True) + 1e-06)


def pick_kernel(returned_ref, code_ref, nearest_ref):
    code = code_ref[...]
    owner = code // 2
    first_slot = code == owner * 2
    values = jnp.where(first_slot, returned_ref[:, :1], returned_ref[:, 127:])
    mine = iota((OWNERS, ROWS), 0) == owner
    nearest_ref[...] = jnp.sum(jnp.where(mine, values, 0.0), axis=0, keepdims=True)


def call(kernel, outs, *operands):
    spec = pl.BlockSpec(memory_space=pltpu.VMEM)
    many = isinstance(outs, list)
    return pl.pallas_call(
        kernel,
        out_shape=outs,
        in_specs=[spec] * len(operands),
        out_specs=[spec] * len(outs) if many else spec,
        compiler_params=VMEM,
    )(*operands)


def exchange(value):
    return lax.all_to_all(value, "clus", split_axis=0, concat_axis=0, tiled=True)


def on_device(embeddings, cluster):
    shape = jax.ShapeDtypeStruct
    unit, rest, code = call(
        place_kernel,
        [
            shape((SLOTS, WIDE), jnp.bfloat16),
            shape((SLOTS, DIM), jnp.bfloat16),
            shape((1, ROWS), jnp.int32),
        ],
        embeddings,
        cluster.reshape(1, ROWS),
    )
    unit = exchange(unit)
    rest = exchange(rest)
    others = [
        lax.ppermute(unit, "src", [(i, (i + step) % 4) for i in range(4)]) for step in (3, 1, 2)
    ]
    best = call(score_kernel, shape((OWNERS, 128), jnp.float32), unit, *others)
    returned = exchange(best)
    partial = call(sum_kernel, shape((CLUS_DEV, DIM), jnp.float32), unit, rest)
    parts = lax.all_gather(partial, "src", axis=0, tiled=True)
    centroids = call(centroid_kernel, shape((CLUS_DEV, DIM), jnp.float32), parts)
    nearest = call(pick_kernel, shape((1, ROWS), jnp.float32), returned, code)
    return centroids, nearest.reshape(ROWS)


def solution(mesh):
    return jax.shard_map(
        on_device,
        mesh=mesh,
        in_specs=(P(("clus", "src"), None), P(("clus", "src"))),
        out_specs=(P("clus", None), P(("clus", "src"))),
        check_vma=False,
    )
```

time: 127 us -> 121 us (0.953)
  blocking collectives: 92.2 us -> 10.1 us
  starting transfers between devices: 11.3 us -> 57.3 us
  waiting for transfers between devices: 13.2 us -> 44.9 us
  Pallas kernels: 7.55 us -> 4.06 us
  local copies, waits for them, and re-layouts: 1.64 us -> 3.81 us
    all_to_all x2 -> x0, blocking collectives: 92.2 us -> none  [the longest x1 66.7 us: on_device(): lax.all_to_all(sent, 'clus', split_axis=0, concat_axis=0, tiled=True)]
    all_to_all x0 -> x3, starting transfers between devices: none -> 46 us  [exchange(): lax.all_to_all(value, 'clus', split_axis=0, concat_axis=0, tiled=True)]
    all_to_all x0 -> x3, waiting for transfers between devices: none -> 30.6 us  [exchange(): lax.all_to_all(value, 'clus', split_axis=0, concat_axis=0, tiled=True)]
    all_gather x0 -> x1, blocking collectives: none -> 10.1 us  [on_device(): parts = lax.all_gather(partial, 'src', axis=0, tiled=True)]
    pallas_call x4 -> x5, Pallas kernels: 7.55 us -> 4.06 us  [call(): pl.pallas_call(kernel, out_shape=outs, in_specs=[spec] * len(operands), o...]
    all_to_all x0 -> x4, local copies, waits for them, and re-layouts: none -> 2.17 us  [exchange(): lax.all_to_all(value, 'clus', split_axis=0, concat_axis=0, tiled=True)]
  transfers between devices with their start and end apart: 3 -> 6, of which waited for: 2 -> 4; matrix products, arithmetic and copies ran while one was open for 0% -> 0% of each run, Pallas kernels for 0% -> 2%
where the time goes in v2:
time: 121 us
  starting transfers between devices  57.3 us (47%)
  waiting for transfers between devices  44.9 us (37%)
  blocking collectives  10.1 us (8%)
  Pallas kernels  4.06 us (3%)
  local copies, waits for them, and re-layouts  3.81 us (3%)
    all_to_all x3, starting transfers between devices, exchange(): lax.all_to_all(value, 'clus', split_axis=0, concat_axis=0, tiled=True)  46 us
    all_to_all x3, waiting for transfers between devices, exchange(): lax.all_to_all(value, 'clus', split_axis=0, concat_axis=0, tiled=True)  30.6 us
    ppermute x3, waiting for transfers between devices, on_device(): lax.ppermute(unit, 'src', [(i, (i + step) % 4) for i in range(4)])  14.3 us
    ppermute x3, starting transfers between devices, on_device(): lax.ppermute(unit, 'src', [(i, (i + step) % 4) for i in range(4)])  11.3 us
    all_gather x1, blocking collectives, on_device(): parts = lax.all_gather(partial, 'src', axis=0, tiled=True)  10.1 us
    pallas_call x5, Pallas kernels, call(): pl.pallas_call(kernel, out_shape=outs, in_specs=[spec] * len(operands), o...  4.06 us
  transfers between devices with their start and end apart: 6, of which 4 were waited for; matrix products, arithmetic and copies ran while one was open for 0% of the time, Pallas kernels for 2%

profile of v2, /device:TPU:1, one launch (start us, length us, event | category | flops | bytes accessed | tf_op | source)
XLA Modules:
  0.0 120.9 jit_solution(15296363209021914096)
XLA Ops:
  0.6 0.6 copy-done.1
  1.3 1.0 copy-done
  2.3 0.5 shard_map.41
  2.8 0.9 all_to_all.21
  3.8 20.4 %all-to-all-start = ((bf16[128,2,896]{2,1,0:T(2,128)(2,1)}), bf16[128,2,896]{2,1,0:T(2,128)(2,1)S(1)}, u32[]{:S(2)}, u32[]{:S(2)}) async-start(bf16[128,2,896]{2,1,0:T(2,128)(2,1)} %all_to_all.21), calls=%async_computation | async-start | bytes 917504 | tf_op jit(solution)/shard_map/all_to_all | solution.py:141
  24.2 0.9 all_to_all.24
  25.1 27.2 %all-to-all-done = bf16[128,2,896]{2,1,0:T(2,128)(2,1)S(1)} async-done(((bf16[128,2,896]{2,1,0:T(2,128)(2,1)}), bf16[128,2,896]{2,1,0:T(2,128)(2,1)S(1)}, u32[]{:S(2)}, u32[]{:S(2)}) %all-to-all-start) | async-done | bytes 458784 | tf_op jit(solution)/shard_map/all_to_all | solution.py:141
  52.3 9.0 %all-to-all-start.1 = ((bf16[128,2,768]{2,1,0:T(2,128)(2,1)}), bf16[128,2,768]{2,1,0:T(2,128)(2,1)S(1)}, u32[]{:S(2)}, u32[]{:S(2)}) async-start(bf16[128,2,768]{2,1,0:T(2,128)(2,1)} %all_to_all.24), calls=%async_computation.1 | async-start | bytes 786432 | tf_op jit(solution)/shard_map/all_to_all | solution.py:141
  61.3 0.2 all_to_all.23.unit_ref.own_ref
  61.5 4.8 %collective-permute-start.2 = (bf16[256,896]{1,0:T(8,128)(2,1)S(1)}, bf16[256,896]{1,0:T(8,128)(2,1)S(1)}, u32[]{:S(2)}, u32[]{:S(2)}) collective-permute-start(bf16[256,896]{1,0:T(8,128)(2,1)S(1)} %all_to_all.23.unit_ref.own_ref), channel_id=1, source_target_pairs={{0,2},{1,3},{2,0},{3,1},{4,6},{5,7},{6,4},{7,5},{8,10},{9,11},{10,... | collective-permute-start | bytes 1376264 | tf_op jit(solution)/shard_map/ppermute | solution.py:159
  66.3 2.3 %collective-permute-start.1 = (bf16[256,896]{1,0:T(8,128)(2,1)S(1)}, bf16[256,896]{1,0:T(8,128)(2,1)S(1)}, u32[]{:S(2)}, u32[]{:S(2)}) collective-permute-start(bf16[256,896]{1,0:T(8,128)(2,1)S(1)} %all_to_all.23.unit_ref.own_ref), channel_id=1, source_target_pairs={{0,1},{1,2},{2,3},{3,0},{4,5},{5,6},{6,7},{7,4},{8,9},{9,10},{10,1... | collective-permute-start | bytes 1376264 | tf_op jit(solution)/shard_map/ppermute | solution.py:159
  68.7 4.2 %collective-permute-start = (bf16[256,896]{1,0:T(8,128)(2,1)S(1)}, bf16[256,896]{1,0:T(8,128)(2,1)S(1)}, u32[]{:S(2)}, u32[]{:S(2)}) collective-permute-start(bf16[256,896]{1,0:T(8,128)(2,1)S(1)} %all_to_all.23.unit_ref.own_ref), channel_id=1, source_target_pairs={{0,3},{1,0},{2,1},{3,2},{4,7},{5,4},{6,5},{7,6},{8,11},{9,8},{10,9... | collective-permute-start | bytes 1376264 | tf_op jit(solution)/shard_map/ppermute | solution.py:159
  72.9 3.2 %collective-permute-done.2.across_ref = bf16[256,896]{1,0:T(8,128)(2,1)S(1)} collective-permute-done((bf16[256,896]{1,0:T(8,128)(2,1)S(1)}, bf16[256,896]{1,0:T(8,128)(2,1)S(1)}, u32[]{:S(2)}, u32[]{:S(2)}) %collective-permute-start.2) | collective-permute-done | bytes 458784 | tf_op jit(solution)/shard_map/ppermute | solution.py:159
  76.1 11.1 %collective-permute-done.1.last_ref = bf16[256,896]{1,0:T(8,128)(2,1)S(1)} collective-permute-done((bf16[256,896]{1,0:T(8,128)(2,1)S(1)}, bf16[256,896]{1,0:T(8,128)(2,1)S(1)}, u32[]{:S(2)}, u32[]{:S(2)}) %collective-permute-start.1) | collective-permute-done | bytes 458784 | tf_op jit(solution)/shard_map/ppermute | solution.py:159
  87.2 0.0 collective-permute-done.next_ref
  87.2 1.6 %shard_map.44 = f32[128,128]{1,0:T(8,128)} custom-call(bf16[256,896]{1,0:T(8,128)(2,1)S(1)} %all_to_all.23.unit_ref.own_ref, bf16[256,896]{1,0:T(8,128)(2,1)S(1)} %collective-permute-done.next_ref, bf16[256,896]{1,0:T(8,128)(2,1)S(1)} %collective-permute-done.1.last_ref, bf16[256,896]{1,0:T(8,128)(2,1)S(1)} %collective-permute-done.2.across_ref), custom_call_target="tpu_custom_call" | custom-call | tf_op jit(solution)/shard_map/pallas_call | solution.py:131
  88.8 0.0 all-to-all-done.1
  88.8 16.6 %all-to-all-start.2 = ((f32[128,1,128]{2,1,0:T(1,128)}), f32[128,1,128]{2,1,0:T(1,128)S(1)}, u32[]{:S(2)}, u32[]{:S(2)}) async-start(f32[128,1,128]{2,1,0:T(1,128)} %bitcast.2), calls=%async_computation.2 | async-start | bytes 131072 | tf_op jit(solution)/shard_map/all_to_all | solution.py:141
  105.5 0.1 all_to_all.26.rest_ref
  105.6 0.5 shard_map.42
  106.2 10.1 %all_gather.3.parts_ref = f32[32,768]{1,0:T(8,128)S(1)} all-gather(f32[8,768]{1,0:T(8,128)S(1)} %shard_map.42), channel_id=1, replica_groups=mesh['clus'=128,'src'=4] {'src'}, dimensions={0}, use_global_device_ids=true | all-gather | bytes 122880 | tf_op jit(solution)/shard_map/all_gather | solution.py:164
  116.2 0.7 shard_map.43
  116.9 3.4 %all-to-all-done.2 = f32[128,1,128]{2,1,0:T(1,128)S(1)} async-done(((f32[128,1,128]{2,1,0:T(1,128)}), f32[128,1,128]{2,1,0:T(1,128)S(1)}, u32[]{:S(2)}, u32[]{:S(2)}) %all-to-all-start.2) | async-done | bytes 65568 | tf_op jit(solution)/shard_map/all_to_all | solution.py:141
  120.3 0.6 shard_map.45
  (2 shorter events, 0.0 us)
Async XLA Ops:
  0.6 0.7 copy-start.1
  1.3 1.0 copy-start
  3.8 48.5 %all-to-all-start = ((bf16[128,2,896]{2,1,0:T(2,128)(2,1)}), bf16[128,2,896]{2,1,0:T(2,128)(2,1)S(1)}, u32[]{:S(2)}, u32[]{:S(2)}) async-start(bf16[128,2,896]{2,1,0:T(2,128)(2,1)} %all_to_all.21), calls=%async_computation | async-start | bytes 917504 | tf_op jit(solution)/shard_map/all_to_all | solution.py:141
  52.3 36.5 %all-to-all-start.1 = ((bf16[128,2,768]{2,1,0:T(2,128)(2,1)}), bf16[128,2,768]{2,1,0:T(2,128)(2,1)S(1)}, u32[]{:S(2)}, u32[]{:S(2)}) async-start(bf16[128,2,768]{2,1,0:T(2,128)(2,1)} %all_to_all.24), calls=%async_computation.1 | async-start | bytes 786432 | tf_op jit(solution)/shard_map/all_to_all | solution.py:141
  61.5 14.6 %collective-permute-start.2 = (bf16[256,896]{1,0:T(8,128)(2,1)S(1)}, bf16[256,896]{1,0:T(8,128)(2,1)S(1)}, u32[]{:S(2)}, u32[]{:S(2)}) collective-permute-start(bf16[256,896]{1,0:T(8,128)(2,1)S(1)} %all_to_all.23.unit_ref.own_ref), channel_id=1, source_target_pairs={{0,2},{1,3},{2,0},{3,1},{4,6},{5,7},{6,4},{7,5},{8,10},{9,11},{10,... | collective-permute-start | bytes 1376264 | tf_op jit(solution)/shard_map/ppermute | solution.py:159
  66.3 20.8 %collective-permute-start.1 = (bf16[256,896]{1,0:T(8,128)(2,1)S(1)}, bf16[256,896]{1,0:T(8,128)(2,1)S(1)}, u32[]{:S(2)}, u32[]{:S(2)}) collective-permute-start(bf16[256,896]{1,0:T(8,128)(2,1)S(1)} %all_to_all.23.unit_ref.own_ref), channel_id=1, source_target_pairs={{0,1},{1,2},{2,3},{3,0},{4,5},{5,6},{6,7},{7,4},{8,9},{9,10},{10,1... | collective-permute-start | bytes 1376264 | tf_op jit(solution)/shard_map/ppermute | solution.py:159
  68.7 18.5 %collective-permute-start = (bf16[256,896]{1,0:T(8,128)(2,1)S(1)}, bf16[256,896]{1,0:T(8,128)(2,1)S(1)}, u32[]{:S(2)}, u32[]{:S(2)}) collective-permute-start(bf16[256,896]{1,0:T(8,128)(2,1)S(1)} %all_to_all.23.unit_ref.own_ref), channel_id=1, source_target_pairs={{0,3},{1,0},{2,1},{3,2},{4,7},{5,4},{6,5},{7,6},{8,11},{9,8},{10,9... | collective-permute-start | bytes 1376264 | tf_op jit(solution)/shard_map/ppermute | solution.py:159
  88.8 31.5 %all-to-all-start.2 = ((f32[128,1,128]{2,1,0:T(1,128)}), f32[128,1,128]{2,1,0:T(1,128)S(1)}, u32[]{:S(2)}, u32[]{:S(2)}) async-start(f32[128,1,128]{2,1,0:T(1,128)} %bitcast.2), calls=%async_computation.2 | async-start | bytes 131072 | tf_op jit(solution)/shard_map/all_to_all | solution.py:141

commit v3 on v2

v3 whole, which is shorter than its diff:
```python
import jax
import jax.numpy as jnp
from jax import lax
from jax.experimental import pallas as pl
from jax.experimental.pallas import tpu as pltpu
from jax.sharding import PartitionSpec as P

CLUS_DEV = 8
OWNERS = 128
ROWS = 128
SLOTS = 256
DIM = 768
WIDE = DIM + 128
GROUPS = DIM // 128
LEAST_POWER = -3520.0
EDGE = 3.38e38
VMEM = pltpu.CompilerParams(vmem_limit_bytes=48 * 1024 * 1024)


def narrow(value):
    return jnp.clip(value, -EDGE, EDGE).astype(jnp.bfloat16)


def pieces(value):
    high = narrow(value)
    rest = value - high.astype(jnp.float32)
    middle = rest.astype(jnp.bfloat16)
    low = (rest - middle.astype(jnp.float32)).astype(jnp.bfloat16)
    return high, middle, low


def product(left, right, contract):
    return lax.dot_general(
        left, right, (contract, ((), ())), preferred_element_type=jnp.float32
    )


def iota(shape, dimension):
    return lax.broadcasted_iota(jnp.int32, shape, dimension)


def stored(high, low):
    return (high * 256.0 + low).astype(jnp.int32).astype(jnp.int16)


def place_kernel(rows_ref, cluster_ref, sent_ref, code_ref):
    cluster = cluster_ref[...]
    owner = cluster // CLUS_DEV
    label = cluster - owner * CLUS_DEV
    first = iota((OWNERS, ROWS), 0)
    second = iota((OWNERS, ROWS), 1)
    hits = first == owner
    earlier = product(
        hits.astype(jnp.bfloat16), (first < second).astype(jnp.bfloat16), ((1,), (0,))
    )
    position = jnp.sum(jnp.where(hits & (earlier > 0.5), 1, 0), axis=0, keepdims=True)
    code = owner * 2 + position
    code_ref[...] = code
    chosen = (iota((SLOTS, ROWS), 0) == code).astype(jnp.bfloat16)

    def placed(steps):
        high = jnp.floor(steps * (1.0 / 256.0) + 0.5)
        low = steps - high * 256.0
        return (
            product(chosen, high.astype(jnp.bfloat16), ((1,), (0,))),
            product(chosen, low.astype(jnp.bfloat16), ((1,), (0,))),
        )

    powers = jnp.zeros((ROWS, 128), jnp.float32)
    for group in range(GROUPS):
        here = slice(group * 128, (group + 1) * 128)
        values = rows_ref[:, here]
        most = jnp.max(jnp.abs(values), axis=1, keepdims=True)
        power = jnp.clip(jnp.ceil(jnp.log2(most) * 32.0), LEAST_POWER, 4096.0)
        steps = jnp.round(values * jnp.exp2(15.0 - power * (1.0 / 32.0)))
        sent_ref[:, here] = stored(*placed(jnp.clip(steps, -32767.0, 32767.0)))
        powers = jnp.where(second == CLUS_DEV + group, power, powers)
    labels = (first == label).astype(jnp.bfloat16)
    high, low = placed(powers)
    sent_ref[:, DIM:] = stored(high, low + product(chosen, labels, ((1,), (1,))))


def decoded(ref):
    tail = ref[:, DIM:].astype(jnp.float32)
    member = jnp.where(iota((SLOTS, 128), 1) < CLUS_DEV, tail, 0.0).astype(jnp.bfloat16)
    step = jnp.exp2(tail * (1.0 / 32.0) - 15.0)
    rows = [
        ref[:, group * 128 : (group + 1) * 128].astype(jnp.float32)
        * step[:, CLUS_DEV + group : CLUS_DEV + group + 1]
        for group in range(GROUPS)
    ]
    return member, rows


def unit_of(rows):
    square = rows[0] * rows[0]
    for values in rows[1:]:
        square = square + values * values
    scale = lax.rsqrt(jnp.sum(square, axis=1, keepdims=True) + 1e-06)
    return jnp.concatenate([(values * scale).astype(jnp.bfloat16) for values in rows], axis=1)


def score_kernel(own_ref, next_ref, last_ref, across_ref, best_ref):
    not_self = iota((SLOTS, SLOTS), 0) != iota((SLOTS, SLOTS), 1)
    best = jnp.full((SLOTS, SLOTS), -1.0, jnp.float32)
    for ref in (own_ref, next_ref, last_ref, across_ref):
        member, rows = decoded(ref)
        unit = unit_of(rows)
        if ref is own_ref:
            own, own_member = unit, member
        scores = product(own, unit, ((1,), (1,)))
        allowed = product(own_member, member, ((1,), (1,))) > 0.5
        if ref is own_ref:
            allowed = allowed & not_self
        best = jnp.maximum(best, jnp.where(allowed, scores, -1.0))
    most = jnp.max(best, axis=1, keepdims=True)
    slot, lane = iota((SLOTS, 128), 0), iota((SLOTS, 128), 1)
    spread = jnp.where((lane < 64) == (slot % 2 == 0), most, 0.0)
    pair = (iota((OWNERS, SLOTS), 1) // 2 == iota((OWNERS, SLOTS), 0)).astype(jnp.bfloat16)
    high, middle, low = [product(pair, piece, ((1,), (0,))) for piece in pieces(spread)]
    best_ref[...] = (high + middle) + low


def centroid_kernel(own_ref, next_ref, last_ref, across_ref, centroid_ref):
    parts = []
    for ref in (own_ref, next_ref, last_ref, across_ref):
        member, rows = decoded(ref)
        high, middle, low = [
            product(member, piece, ((0,), (0,)))[:CLUS_DEV]
            for piece in pieces(jnp.concatenate(rows, axis=1))
        ]
        parts.append((high + middle) + low)
    sums = (parts[0] + parts[3]) + (parts[1] + parts[2])
    centroid_ref[...] = sums * lax.rsqrt(jnp.sum(sums * sums, axis=1, keepdims=True) + 1e-06)


def pick_kernel(returned_ref, code_ref, nearest_ref):
    code = code_ref[...]
    owner = code // 2
    first_slot = code == owner * 2
    values = jnp.where(first_slot, returned_ref[:, :1], returned_ref[:, 127:])
    mine = iota((OWNERS, ROWS), 0) == owner
    nearest_ref[...] = jnp.sum(jnp.where(mine, values, 0.0), axis=0, keepdims=True)


def call(kernel, outs, *operands):
    spec = pl.BlockSpec(memory_space=pltpu.VMEM)
    many = isinstance(outs, list)
    return pl.pallas_call(
        kernel,
        out_shape=outs,
        in_specs=[spec] * len(operands),
        out_specs=[spec] * len(outs) if many else spec,
        compiler_params=VMEM,
    )(*operands)


def exchange(value):
    return lax.all_to_all(value, "clus", split_axis=0, concat_axis=0, tiled=True)


def on_device(embeddings, cluster):
    shape = jax.ShapeDtypeStruct
    sent, code = call(
        place_kernel,
        [shape((SLOTS, WIDE), jnp.int16), shape((1, ROWS), jnp.int32)],
        embeddings,
        cluster.reshape(1, ROWS),
    )
    block = exchange(sent)
    blocks = [block] + [
        lax.ppermute(block, "src", [(i, (i + step) % 4) for i in range(4)]) for step in (3, 1, 2)
    ]
    best = call(score_kernel, shape((OWNERS, 128), jnp.float32), *blocks)
    returned = exchange(best)
    centroids = call(centroid_kernel, shape((CLUS_DEV, DIM), jnp.float32), *blocks)
    nearest = call(pick_kernel, shape((1, ROWS), jnp.float32), returned, code)
    return centroids, nearest.reshape(ROWS)


def solution(mesh):
    return jax.shard_map(
        on_device,
        mesh=mesh,
        in_specs=(P(("clus", "src"), None), P(("clus", "src"))),
        out_specs=(P("clus", None), P(("clus", "src"))),
        check_vma=False,
    )
```

time: 121 us -> 106 us (0.88)
  blocking collectives: 10.1 us -> 48.3 us
  starting transfers between devices: 57.3 us -> 20.4 us
  waiting for transfers between devices: 44.9 us -> 27 us
  Pallas kernels: 4.06 us -> 7.02 us
  local copies, waits for them, and re-layouts: 3.81 us -> 2.03 us
    all_to_all x0 -> x1, blocking collectives: none -> 48.3 us  [exchange(): lax.all_to_all(value, 'clus', split_axis=0, concat_axis=0, tiled=True)]
    all_to_all x3 -> x1, starting transfers between devices: 46 us -> 9.07 us  [exchange(): lax.all_to_all(value, 'clus', split_axis=0, concat_axis=0, tiled=True)]
    all_to_all x3 -> x1, waiting for transfers between devices: 30.6 us -> 12.6 us  [exchange(): lax.all_to_all(value, 'clus', split_axis=0, concat_axis=0, tiled=True)]
    all_gather x1 -> x0, blocking collectives: 10.1 us -> none  [on_device(): parts = lax.all_gather(partial, 'src', axis=0, tiled=True)]
    pallas_call x5 -> x4, Pallas kernels: 4.06 us -> 7.02 us  [call(): pl.pallas_call(kernel, out_shape=outs, in_specs=[spec] * len(operands), o...]
    all_to_all x4 -> x2, local copies, waits for them, and re-layouts: 2.17 us -> 0.38 us  [exchange(): lax.all_to_all(value, 'clus', split_axis=0, concat_axis=0, tiled=True)]
  transfers between devices with their start and end apart: 6 -> 4, of which waited for: 4 -> 3; matrix products, arithmetic and copies ran while one was open for 0% -> 0% of each run, Pallas kernels for 2% -> 2%
where the time goes in v3:
time: 106 us; the launch traced here: 105 us
  blocking collectives  48.3 us (46%)
  waiting for transfers between devices  27 us (25%)
  starting transfers between devices  20.4 us (19%)
  Pallas kernels  7.02 us (7%)
  local copies, waits for them, and re-layouts  2.03 us (2%)
    all_to_all x1, blocking collectives, exchange(): lax.all_to_all(value, 'clus', split_axis=0, concat_axis=0, tiled=True)  48.3 us
    ppermute x3, waiting for transfers between devices, on_device(): lax.ppermute(block, 'src', [(i, (i + step) % 4) for i in range(4)])  14.3 us
    all_to_all x1, waiting for transfers between devices, exchange(): lax.all_to_all(value, 'clus', split_axis=0, concat_axis=0, tiled=True)  12.6 us
    ppermute x3, starting transfers between devices, on_device(): lax.ppermute(block, 'src', [(i, (i + step) % 4) for i in range(4)])  11.3 us
    all_to_all x1, starting transfers between devices, exchange(): lax.all_to_all(value, 'clus', split_axis=0, concat_axis=0, tiled=True)  9.07 us
    pallas_call x4, Pallas kernels, call(): pl.pallas_call(kernel, out_shape=outs, in_specs=[spec] * len(operands), o...  7.02 us
  transfers between devices with their start and end apart: 4, of which 3 were waited for; matrix products, arithmetic and copies ran while one was open for 0% of the time, Pallas kernels for 2%

profile of v3, /device:TPU:1, one launch (start us, length us, event | category | flops | bytes accessed | tf_op | source)
XLA Modules:
  0.0 105.4 jit_solution(11368976973063890790)
XLA Ops:
  0.6 0.0 copy-start.1
  0.6 0.6 copy-done.1
  1.3 0.0 copy-start
  1.3 1.0 copy-done
  2.3 0.6 shard_map.41
  2.9 0.2 all_to_all.14
  3.1 48.3 %all_to_all.22 = s16[128,2,896]{2,1,0:T(2,128)(2,1)S(1)} all-to-all(s16[128,2,896]{2,1,0:T(2,128)(2,1)S(1)} %all_to_all.14), channel_id=1, replica_groups=mesh['clus'=128,'src'=4] {'clus'}, dimensions={0} | all-to-all | bytes 917504 | tf_op jit(solution)/shard_map/all_to_all | solution.py:159
  51.4 0.2 all_to_all.16.own_ref
  51.6 4.8 %collective-permute-start.2 = (s16[256,896]{1,0:T(8,128)(2,1)S(1)}, s16[256,896]{1,0:T(8,128)(2,1)S(1)}, u32[]{:S(2)}, u32[]{:S(2)}) collective-permute-start(s16[256,896]{1,0:T(8,128)(2,1)S(1)} %all_to_all.16.own_ref), channel_id=1, source_target_pairs={{0,2},{1,3},{2,0},{3,1},{4,6},{5,7},{6,4},{7,5},{8,10},{9,11},{10,... | collective-permute-start | bytes 1376264 | tf_op jit(solution)/shard_map/ppermute | solution.py:172
  56.5 2.3 %collective-permute-start.1 = (s16[256,896]{1,0:T(8,128)(2,1)S(1)}, s16[256,896]{1,0:T(8,128)(2,1)S(1)}, u32[]{:S(2)}, u32[]{:S(2)}) collective-permute-start(s16[256,896]{1,0:T(8,128)(2,1)S(1)} %all_to_all.16.own_ref), channel_id=1, source_target_pairs={{0,1},{1,2},{2,3},{3,0},{4,5},{5,6},{6,7},{7,4},{8,9},{9,10},{10,1... | collective-permute-start | bytes 1376264 | tf_op jit(solution)/shard_map/ppermute | solution.py:172
  58.8 4.2 %collective-permute-start = (s16[256,896]{1,0:T(8,128)(2,1)S(1)}, s16[256,896]{1,0:T(8,128)(2,1)S(1)}, u32[]{:S(2)}, u32[]{:S(2)}) collective-permute-start(s16[256,896]{1,0:T(8,128)(2,1)S(1)} %all_to_all.16.own_ref), channel_id=1, source_target_pairs={{0,3},{1,0},{2,1},{3,2},{4,7},{5,4},{6,5},{7,6},{8,11},{9,8},{10,9... | collective-permute-start | bytes 1376264 | tf_op jit(solution)/shard_map/ppermute | solution.py:172
  63.0 3.1 %collective-permute-done.2.across_ref = s16[256,896]{1,0:T(8,128)(2,1)S(1)} collective-permute-done((s16[256,896]{1,0:T(8,128)(2,1)S(1)}, s16[256,896]{1,0:T(8,128)(2,1)S(1)}, u32[]{:S(2)}, u32[]{:S(2)}) %collective-permute-start.2) | collective-permute-done | bytes 458784 | tf_op jit(solution)/shard_map/ppermute | solution.py:172
  66.0 11.3 %collective-permute-done.1.last_ref = s16[256,896]{1,0:T(8,128)(2,1)S(1)} collective-permute-done((s16[256,896]{1,0:T(8,128)(2,1)S(1)}, s16[256,896]{1,0:T(8,128)(2,1)S(1)}, u32[]{:S(2)}, u32[]{:S(2)}) %collective-permute-start.1) | collective-permute-done | bytes 458784 | tf_op jit(solution)/shard_map/ppermute | solution.py:172
  77.3 0.0 collective-permute-done.next_ref
  77.3 3.5 %shard_map.43 = f32[128,128]{1,0:T(8,128)} custom-call(s16[256,896]{1,0:T(8,128)(2,1)S(1)} %all_to_all.16.own_ref, s16[256,896]{1,0:T(8,128)(2,1)S(1)} %collective-permute-done.next_ref, s16[256,896]{1,0:T(8,128)(2,1)S(1)} %collective-permute-done.1.last_ref, s16[256,896]{1,0:T(8,128)(2,1)S(1)} %collective-permute-done.2.across_ref), custom_call_target="tpu_custom_call" | custom-call | tf_op jit(solution)/shard_map/pallas_call | solution.py:149
  80.8 9.1 %all-to-all-start.1 = ((f32[128,1,128]{2,1,0:T(1,128)}), f32[128,1,128]{2,1,0:T(1,128)S(1)}, u32[]{:S(2)}, u32[]{:S(2)}) async-start(f32[128,1,128]{2,1,0:T(1,128)} %bitcast.2), calls=%async_computation.1 | async-start | bytes 131072 | tf_op jit(solution)/shard_map/all_to_all | solution.py:159
  89.9 2.3 %shard_map.42 = f32[8,768]{1,0:T(8,128)} custom-call(s16[256,896]{1,0:T(8,128)(2,1)S(1)} %all_to_all.16.own_ref, s16[256,896]{1,0:T(8,128)(2,1)S(1)} %collective-permute-done.next_ref, s16[256,896]{1,0:T(8,128)(2,1)S(1)} %collective-permute-done.1.last_ref, s16[256,896]{1,0:T(8,128)(2,1)S(1)} %collective-permute-done.2.across_ref), custom_call_target="tpu_custom_call" | custom-call | tf_op jit(solution)/shard_map/pallas_call | solution.py:149
  92.2 12.6 %all-to-all-done.1 = f32[128,1,128]{2,1,0:T(1,128)S(1)} async-done(((f32[128,1,128]{2,1,0:T(1,128)}), f32[128,1,128]{2,1,0:T(1,128)S(1)}, u32[]{:S(2)}, u32[]{:S(2)}) %all-to-all-start.1) | async-done | bytes 65568 | tf_op jit(solution)/shard_map/all_to_all | solution.py:159
  104.8 0.6 shard_map.44
Async XLA Ops:
  0.6 0.7 copy-start.1
  1.3 1.0 copy-start
  51.6 14.4 %collective-permute-start.2 = (s16[256,896]{1,0:T(8,128)(2,1)S(1)}, s16[256,896]{1,0:T(8,128)(2,1)S(1)}, u32[]{:S(2)}, u32[]{:S(2)}) collective-permute-start(s16[256,896]{1,0:T(8,128)(2,1)S(1)} %all_to_all.16.own_ref), channel_id=1, source_target_pairs={{0,2},{1,3},{2,0},{3,1},{4,6},{5,7},{6,4},{7,5},{8,10},{9,11},{10,... | collective-permute-start | bytes 1376264 | tf_op jit(solution)/shard_map/ppermute | solution.py:172
  56.5 20.8 %collective-permute-start.1 = (s16[256,896]{1,0:T(8,128)(2,1)S(1)}, s16[256,896]{1,0:T(8,128)(2,1)S(1)}, u32[]{:S(2)}, u32[]{:S(2)}) collective-permute-start(s16[256,896]{1,0:T(8,128)(2,1)S(1)} %all_to_all.16.own_ref), channel_id=1, source_target_pairs={{0,1},{1,2},{2,3},{3,0},{4,5},{5,6},{6,7},{7,4},{8,9},{9,10},{10,1... | collective-permute-start | bytes 1376264 | tf_op jit(solution)/shard_map/ppermute | solution.py:172
  58.8 18.5 %collective-permute-start = (s16[256,896]{1,0:T(8,128)(2,1)S(1)}, s16[256,896]{1,0:T(8,128)(2,1)S(1)}, u32[]{:S(2)}, u32[]{:S(2)}) collective-permute-start(s16[256,896]{1,0:T(8,128)(2,1)S(1)} %all_to_all.16.own_ref), channel_id=1, source_target_pairs={{0,3},{1,0},{2,1},{3,2},{4,7},{5,4},{6,5},{7,6},{8,11},{9,8},{10,9... | collective-permute-start | bytes 1376264 | tf_op jit(solution)/shard_map/ppermute | solution.py:172
  80.8 24.0 %all-to-all-start.1 = ((f32[128,1,128]{2,1,0:T(1,128)}), f32[128,1,128]{2,1,0:T(1,128)S(1)}, u32[]{:S(2)}, u32[]{:S(2)}) async-start(f32[128,1,128]{2,1,0:T(1,128)} %bitcast.2), calls=%async_computation.1 | async-start | bytes 131072 | tf_op jit(solution)/shard_map/all_to_all | solution.py:159

commit v4 on v3

--- a/solution.py
+++ b/solution.py
@@ -80,39 +80,41 @@
     sent_ref[:, DIM:] = stored(high, low + product(chosen, labels, ((1,), (1,))))
 
 
-def decoded(ref):
-    tail = ref[:, DIM:].astype(jnp.float32)
+def decoded(ref, start):
+    here = slice(start, start + SLOTS)
+    tail = ref[here, DIM:].astype(jnp.float32)
     member = jnp.where(iota((SLOTS, 128), 1) < CLUS_DEV, tail, 0.0).astype(jnp.bfloat16)
     step = jnp.exp2(tail * (1.0 / 32.0) - 15.0)
     rows = [
-        ref[:, group * 128 : (group + 1) * 128].astype(jnp.float32)
+        ref[here, group * 128 : (group + 1) * 128].astype(jnp.float32)
         * step[:, CLUS_DEV + group : CLUS_DEV + group + 1]
         for group in range(GROUPS)
     ]
     return member, rows
 
 
-def unit_of(rows):
-    square = rows[0] * rows[0]
-    for values in rows[1:]:
-        square = square + values * values
-    scale = lax.rsqrt(jnp.sum(square, axis=1, keepdims=True) + 1e-06)
-    return jnp.concatenate([(values * scale).astype(jnp.bfloat16) for values in rows], axis=1)
-
-
-def score_kernel(own_ref, next_ref, last_ref, across_ref, best_ref):
-    not_self = iota((SLOTS, SLOTS), 0) != iota((SLOTS, SLOTS), 1)
+def score_kernel(all_ref, best_ref, unit_ref, member_ref):
+    starts = range(0, all_ref.shape[0], SLOTS)
+    for start in starts:
+        member, rows = decoded(all_ref, start)
+        square = rows[0] * rows[0]
+        for values in rows[1:]:
+            square = square + values * values
+        scale = lax.rsqrt(jnp.sum(square, axis=1, keepdims=True) + 1e-06)
+        here = slice(start, start + SLOTS)
+        for group, values in enumerate(rows):
+            unit_ref[here, group * 128 : (group + 1) * 128] = (values * scale).astype(jnp.bfloat16)
+        member_ref[here, :] = member
+    offset = pl.multiple_of(lax.axis_index("src") * SLOTS, SLOTS)
+    own = unit_ref[pl.ds(offset, SLOTS), :]
+    own_member = member_ref[pl.ds(offset, SLOTS), :]
+    apart = iota((SLOTS, SLOTS), 0) - iota((SLOTS, SLOTS), 1) + offset
     best = jnp.full((SLOTS, SLOTS), -1.0, jnp.float32)
-    for ref in (own_ref, next_ref, last_ref, across_ref):
-        member, rows = decoded(ref)
-        unit = unit_of(rows)
-        if ref is own_ref:
-            own, own_member = unit, member
-        scores = product(own, unit, ((1,), (1,)))
-        allowed = product(own_member, member, ((1,), (1,))) > 0.5
-        if ref is own_ref:
-            allowed = allowed & not_self
-        best = jnp.maximum(best, jnp.where(allowed, scores, -1.0))
+    for start in starts:
+        here = slice(start, start + SLOTS)
+        scores = product(own, unit_ref[here, :], ((1,), (1,)))
+        same = product(own_member, member_ref[here, :], ((1,), (1,))) > 0.5
+        best = jnp.maximum(best, jnp.where(same & (apart != start), scores, -1.0))
     most = jnp.max(best, axis=1, keepdims=True)
     slot, lane = iota((SLOTS, 128), 0), iota((SLOTS, 128), 1)
     spread = jnp.where((lane < 64) == (slot % 2 == 0), most, 0.0)
@@ -121,16 +123,12 @@
     best_ref[...] = (high + middle) + low
 
 
-def centroid_kernel(own_ref, next_ref, last_ref, across_ref, centroid_ref):
-    parts = []
-    for ref in (own_ref, next_ref, last_ref, across_ref):
-        member, rows = decoded(ref)
-        high, middle, low = [
-            product(member, piece, ((0,), (0,)))[:CLUS_DEV]
-            for piece in pieces(jnp.concatenate(rows, axis=1))
-        ]
-        parts.append((high + middle) + low)
-    sums = (parts[0] + parts[3]) + (parts[1] + parts[2])
+def centroid_kernel(all_ref, centroid_ref):
+    sums = jnp.zeros((CLUS_DEV, DIM), jnp.float32)
+    for start in range(0, all_ref.shape[0], SLOTS):
+        member, rows = decoded(all_ref, start)
+        for piece in pieces(jnp.concatenate(rows, axis=1)):
+            sums = sums + product(member, piece, ((0,), (0,)))[:CLUS_DEV]
     centroid_ref[...] = sums * lax.rsqrt(jnp.sum(sums * sums, axis=1, keepdims=True) + 1e-06)
 
 
@@ -143,7 +141,7 @@
     nearest_ref[...] = jnp.sum(jnp.where(mine, values, 0.0), axis=0, keepdims=True)
 
 
-def call(kernel, outs, *operands):
+def call(kernel, outs, *operands, scratch=()):
     spec = pl.BlockSpec(memory_space=pltpu.VMEM)
     many = isinstance(outs, list)
     return pl.pallas_call(
@@ -151,6 +149,7 @@
         out_shape=outs,
         in_specs=[spec] * len(operands),
         out_specs=[spec] * len(outs) if many else spec,
+        scratch_shapes=scratch,
         compiler_params=VMEM,
     )(*operands)
 
@@ -167,13 +166,18 @@
         embeddings,
         cluster.reshape(1, ROWS),
     )
-    block = exchange(sent)
-    blocks = [block] + [
-        lax.ppermute(block, "src", [(i, (i + step) % 4) for i in range(4)]) for step in (3, 1, 2)
-    ]
-    best = call(score_kernel, shape((OWNERS, 128), jnp.float32), *blocks)
+    rows = lax.all_gather(exchange(sent), "src", axis=0, tiled=True)
+    best = call(
+        score_kernel,
+        shape((OWNERS, 128), jnp.float32),
+        rows,
+        scratch=[
+            pltpu.VMEM((rows.shape[0], DIM), jnp.bfloat16),
+            pltpu.VMEM((rows.shape[0], 128), jnp.bfloat16),
+        ],
+    )
     returned = exchange(best)
-    centroids = call(centroid_kernel, shape((CLUS_DEV, DIM), jnp.float32), *blocks)
+    centroids = call(centroid_kernel, shape((CLUS_DEV, DIM), jnp.float32), rows)
     nearest = call(pick_kernel, shape((1, ROWS), jnp.float32), returned, code)
     return centroids, nearest.reshape(ROWS)
 

time: 106 us -> 100 us (0.943)
  blocking collectives: 48.3 us -> 66.3 us
  waiting for transfers between devices: 27 us -> 12.6 us
  starting transfers between devices: 20.4 us -> 11.5 us
    all_gather x0 -> x1, blocking collectives: none -> 18 us  [on_device(): rows = lax.all_gather(exchange(sent), 'src', axis=0, tiled=True)]
    ppermute x3 -> x0, waiting for transfers between devices: 14.3 us -> none  [on_device(): lax.ppermute(block, 'src', [(i, (i + step) % 4) for i in range(4)])]
    ppermute x3 -> x0, starting transfers between devices: 11.3 us -> none  [on_device(): lax.ppermute(block, 'src', [(i, (i + step) % 4) for i in range(4)])]
    all_to_all x1, starting transfers between devices: 9.07 us -> 11.5 us  [exchange(): lax.all_to_all(value, 'clus', split_axis=0, concat_axis=0, tiled=True)]
  transfers between devices with their start and end apart: 4 -> 1, of which waited for: 3 -> 1; matrix products, arithmetic and copies ran while one was open for 0% -> 0% of each run, Pallas kernels for 2% -> 2%
where the time goes in v4:
time: 100 us
  blocking collectives  66.3 us (66%)
  waiting for transfers between devices  12.6 us (13%)
  starting transfers between devices  11.5 us (12%)
  Pallas kernels  6.89 us (7%)
  local copies, waits for them, and re-layouts  2.03 us (2%)
    all_to_all x1, blocking collectives, exchange(): lax.all_to_all(value, 'clus', split_axis=0, concat_axis=0, tiled=True)  48.3 us
    all_gather x1, blocking collectives, on_device(): rows = lax.all_gather(exchange(sent), 'src', axis=0, tiled=True)  18 us
    all_to_all x1, waiting for transfers between devices, exchange(): lax.all_to_all(value, 'clus', split_axis=0, concat_axis=0, tiled=True)  12.6 us
    all_to_all x1, starting transfers between devices, exchange(): lax.all_to_all(value, 'clus', split_axis=0, concat_axis=0, tiled=True)  11.5 us
    pallas_call x4, Pallas kernels, call(): pl.pallas_call(kernel, out_shape=outs, in_specs=[spec] * len(operands), o...  6.89 us
  transfers between devices with their start and end apart: 1, of which 1 were waited for; matrix products, arithmetic and copies ran while one was open for 0% of the time, Pallas kernels for 2%

profile of v4, /device:TPU:1, one launch (start us, length us, event | category | flops | bytes accessed | tf_op | source)
XLA Modules:
  0.0 100.0 jit_solution(13549215839306164519)
XLA Ops:
  0.6 0.0 copy-start
  0.6 1.0 copy-done
  1.6 0.0 copy-start.1
  1.6 0.7 copy-done.1
  2.3 0.6 shard_map.41
  2.9 0.2 all_to_all.15
  3.1 48.3 %all_to_all.23 = s16[128,2,896]{2,1,0:T(2,128)(2,1)S(1)} all-to-all(s16[128,2,896]{2,1,0:T(2,128)(2,1)S(1)} %all_to_all.15), channel_id=1, replica_groups=mesh['clus'=128,'src'=4] {'clus'}, dimensions={0} | all-to-all | bytes 917504 | tf_op jit(solution)/shard_map/all_to_all | solution.py:158
  51.4 0.2 all_to_all.17
  51.6 18.0 %all-gather.1.all_ref = s16[1024,896]{1,0:T(8,128)(2,1)S(1)} all-gather(s16[256,896]{1,0:T(8,128)(2,1)S(1)} %all_to_all.17), channel_id=1, replica_groups=mesh['clus'=128,'src'=4] {'src'}, dimensions={0}, use_global_device_ids=true | all-gather | bytes 2293760 | tf_op jit(solution)/shard_map/all_gather | solution.py:169
  69.6 3.4 %shard_map.43 = f32[128,128]{1,0:T(8,128)} custom-call(s16[1024,896]{1,0:T(8,128)(2,1)S(1)} %all-gather.1.all_ref), custom_call_target="tpu_custom_call" | custom-call | tf_op jit(solution)/shard_map/pallas_call | solution.py:147
  73.0 11.5 %all-to-all-start.1 = ((f32[128,1,128]{2,1,0:T(1,128)}), f32[128,1,128]{2,1,0:T(1,128)S(1)}, u32[]{:S(2)}, u32[]{:S(2)}) async-start(f32[128,1,128]{2,1,0:T(1,128)} %bitcast.2), calls=%async_computation.1 | async-start | bytes 131072 | tf_op jit(solution)/shard_map/all_to_all | solution.py:158
  84.5 2.3 %shard_map.42 = f32[8,768]{1,0:T(8,128)} custom-call(s16[1024,896]{1,0:T(8,128)(2,1)S(1)} %all-gather.1.all_ref), custom_call_target="tpu_custom_call" | custom-call | tf_op jit(solution)/shard_map/pallas_call | solution.py:147
  86.8 12.6 %all-to-all-done.1 = f32[128,1,128]{2,1,0:T(1,128)S(1)} async-done(((f32[128,1,128]{2,1,0:T(1,128)}), f32[128,1,128]{2,1,0:T(1,128)S(1)}, u32[]{:S(2)}, u32[]{:S(2)}) %all-to-all-start.1) | async-done | bytes 65568 | tf_op jit(solution)/shard_map/all_to_all | solution.py:158
  99.4 0.6 shard_map.44
Async XLA Ops:
  0.6 1.0 copy-start
  1.6 0.7 copy-start.1
  73.0 26.4 %all-to-all-start.1 = ((f32[128,1,128]{2,1,0:T(1,128)}), f32[128,1,128]{2,1,0:T(1,128)S(1)}, u32[]{:S(2)}, u32[]{:S(2)}) async-start(f32[128,1,128]{2,1,0:T(1,128)} %bitcast.2), calls=%async_computation.1 | async-start | bytes 131072 | tf_op jit(solution)/shard_map/all_to_all | solution.py:158

commit v5 on v4

--- a/solution.py
+++ b/solution.py
@@ -12,7 +12,12 @@
 DIM = 768
 WIDE = DIM + 128
 GROUPS = DIM // 128
-LEAST_POWER = -3520.0
+HALF = 512
+LEAST_POWER = -2560.0
+COARSE = CLUS_DEV + GROUPS
+POWER = COARSE + 2
+FINE = 2.0**21
+TINY = 1e-37
 EDGE = 3.38e38
 VMEM = pltpu.CompilerParams(vmem_limit_bytes=48 * 1024 * 1024)
 
@@ -66,68 +71,84 @@
             product(chosen, low.astype(jnp.bfloat16), ((1,), (0,))),
         )
 
-    powers = jnp.zeros((ROWS, 128), jnp.float32)
-    for group in range(GROUPS):
+    groups = [rows_ref[:, group * 128 : (group + 1) * 128] for group in range(GROUPS)]
+    square = groups[0] * groups[0]
+    for values in groups[1:]:
+        square = square + values * values
+    scale = lax.rsqrt(jnp.sum(square, axis=1, keepdims=True) + 1e-06)
+    tops = [
+        jnp.log2(jnp.maximum(jnp.max(jnp.abs(values), axis=1, keepdims=True), TINY))
+        for values in groups
+    ]
+    top = tops[0]
+    for other in tops[1:]:
+        top = jnp.maximum(top, other)
+    power = jnp.clip(jnp.ceil(top * 32.0), LEAST_POWER, 4096.0)
+    top = power * (1.0 / 32.0)
+    factor = jnp.where(scale > 0.0, top - 15.0 + jnp.log2(jnp.maximum(scale, TINY)), -250.0)
+    coarse = jnp.round(factor * 128.0)
+    fine = jnp.round((factor - coarse * (1.0 / 128.0)) * FINE)
+    fields = jnp.where(second == POWER, power, 0.0)
+    fields = jnp.where(second == COARSE, coarse, jnp.where(second == COARSE + 1, fine, fields))
+    for group, values in enumerate(groups):
+        below = jnp.clip(jnp.floor(top - tops[group]), 0.0, 30.0)
+        steps = jnp.round(values * jnp.exp2(15.0 - top + below))
         here = slice(group * 128, (group + 1) * 128)
-        values = rows_ref[:, here]
-        most = jnp.max(jnp.abs(values), axis=1, keepdims=True)
-        power = jnp.clip(jnp.ceil(jnp.log2(most) * 32.0), LEAST_POWER, 4096.0)
-        steps = jnp.round(values * jnp.exp2(15.0 - power * (1.0 / 32.0)))
         sent_ref[:, here] = stored(*placed(jnp.clip(steps, -32767.0, 32767.0)))
-        powers = jnp.where(second == CLUS_DEV + group, power, powers)
+        fields = jnp.where(second == CLUS_DEV + group, below, fields)
     labels = (first == label).astype(jnp.bfloat16)
-    high, low = placed(powers)
+    high, low = placed(fields)
     sent_ref[:, DIM:] = stored(high, low + product(chosen, labels, ((1,), (1,))))
 
 
-def decoded(ref, start):
-    here = slice(start, start + SLOTS)
+def fields_of(ref, here):
     tail = ref[here, DIM:].astype(jnp.float32)
-    member = jnp.where(iota((SLOTS, 128), 1) < CLUS_DEV, tail, 0.0).astype(jnp.bfloat16)
-    step = jnp.exp2(tail * (1.0 / 32.0) - 15.0)
-    rows = [
-        ref[here, group * 128 : (group + 1) * 128].astype(jnp.float32)
-        * step[:, CLUS_DEV + group : CLUS_DEV + group + 1]
-        for group in range(GROUPS)
-    ]
-    return member, rows
+    lane = iota(tail.shape, 1)
+    member = jnp.where(lane < CLUS_DEV, tail, 0.0).astype(jnp.bfloat16)
+    group = (lane >= CLUS_DEV) & (lane < CLUS_DEV + GROUPS)
+    below = jnp.where(group, jnp.exp2(-jnp.where(group, tail, 0.0)), 0.0).astype(jnp.bfloat16)
+    spread = iota((128, DIM), 1) // 128 + CLUS_DEV == iota((128, DIM), 0)
+    return tail, member, product(below, spread.astype(jnp.bfloat16), ((1,), (0,)))
 
 
 def score_kernel(all_ref, best_ref, unit_ref, member_ref):
-    starts = range(0, all_ref.shape[0], SLOTS)
-    for start in starts:
-        member, rows = decoded(all_ref, start)
-        square = rows[0] * rows[0]
-        for values in rows[1:]:
-            square = square + values * values
-        scale = lax.rsqrt(jnp.sum(square, axis=1, keepdims=True) + 1e-06)
-        here = slice(start, start + SLOTS)
-        for group, values in enumerate(rows):
-            unit_ref[here, group * 128 : (group + 1) * 128] = (values * scale).astype(jnp.bfloat16)
+    for start in range(0, all_ref.shape[0], HALF):
+        here = slice(start, start + HALF)
+        tail, member, below = fields_of(all_ref, here)
+        factor = jnp.exp2(
+            tail[:, COARSE : COARSE + 1] * (1.0 / 128.0)
+            + tail[:, COARSE + 1 : COARSE + 2] * (1.0 / FINE)
+        )
+        unit_ref[here, :] = (all_ref[here, :DIM].astype(jnp.float32) * (below * factor)).astype(
+            jnp.bfloat16
+        )
         member_ref[here, :] = member
     offset = pl.multiple_of(lax.axis_index("src") * SLOTS, SLOTS)
     own = unit_ref[pl.ds(offset, SLOTS), :]
     own_member = member_ref[pl.ds(offset, SLOTS), :]
-    apart = iota((SLOTS, SLOTS), 0) - iota((SLOTS, SLOTS), 1) + offset
+    apart = iota((SLOTS, SLOTS), 1) - iota((SLOTS, SLOTS), 0) + offset
     best = jnp.full((SLOTS, SLOTS), -1.0, jnp.float32)
-    for start in starts:
+    for start in range(0, all_ref.shape[0], SLOTS):
         here = slice(start, start + SLOTS)
-        scores = product(own, unit_ref[here, :], ((1,), (1,)))
-        same = product(own_member, member_ref[here, :], ((1,), (1,))) > 0.5
+        scores = product(unit_ref[here, :], own, ((1,), (1,)))
+        same = product(member_ref[here, :], own_member, ((1,), (1,))) > 0.5
         best = jnp.maximum(best, jnp.where(same & (apart != start), scores, -1.0))
-    most = jnp.max(best, axis=1, keepdims=True)
-    slot, lane = iota((SLOTS, 128), 0), iota((SLOTS, 128), 1)
-    spread = jnp.where((lane < 64) == (slot % 2 == 0), most, 0.0)
-    pair = (iota((OWNERS, SLOTS), 1) // 2 == iota((OWNERS, SLOTS), 0)).astype(jnp.bfloat16)
-    high, middle, low = [product(pair, piece, ((1,), (0,))) for piece in pieces(spread)]
-    best_ref[...] = (high + middle) + low
+    most = jnp.max(best, axis=0, keepdims=True)
+    slot_of = iota((OWNERS, SLOTS), 1) - iota((OWNERS, SLOTS), 0) * 2
+    first, second = [
+        jnp.sum(jnp.where(slot_of == slot, most, 0.0), axis=1, keepdims=True) for slot in range(2)
+    ]
+    best_ref[...] = jnp.where(iota((OWNERS, 128), 1) < 64, first, second)
 
 
 def centroid_kernel(all_ref, centroid_ref):
     sums = jnp.zeros((CLUS_DEV, DIM), jnp.float32)
     for start in range(0, all_ref.shape[0], SLOTS):
-        member, rows = decoded(all_ref, start)
-        for piece in pieces(jnp.concatenate(rows, axis=1)):
+        here = slice(start, start + SLOTS)
+        tail, member, below = fields_of(all_ref, here)
+        step = jnp.exp2(tail[:, POWER : POWER + 1] * (1.0 / 32.0) - 15.0)
+        rows = all_ref[here, :DIM].astype(jnp.float32) * (below * step)
+        for piece in pieces(rows):
             sums = sums + product(member, piece, ((0,), (0,)))[:CLUS_DEV]
     centroid_ref[...] = sums * lax.rsqrt(jnp.sum(sums * sums, axis=1, keepdims=True) + 1e-06)
 

time: 100 us -> 99.1 us (level)
  Pallas kernels: 6.89 us -> 5.88 us
    pallas_call x4, Pallas kernels: 6.89 us -> 5.88 us  [call(): pl.pallas_call(kernel, out_shape=outs, in_specs=[spec] * len(operands), o...]
where the time goes in v5:
time: 99.1 us; the launch traced here: 98.8 us
  blocking collectives  66.3 us (67%)
  waiting for transfers between devices  12.4 us (13%)
  starting transfers between devices  11.5 us (12%)
  Pallas kernels  5.88 us (6%)
  local copies, waits for them, and re-layouts  2.03 us (2%)
    all_to_all x1, blocking collectives, exchange(): lax.all_to_all(value, 'clus', split_axis=0, concat_axis=0, tiled=True)  48.3 us
    all_gather x1, blocking collectives, on_device(): rows = lax.all_gather(exchange(sent), 'src', axis=0, tiled=True)  18 us
    all_to_all x1, waiting for transfers between devices, exchange(): lax.all_to_all(value, 'clus', split_axis=0, concat_axis=0, tiled=True)  12.4 us
    all_to_all x1, starting transfers between devices, exchange(): lax.all_to_all(value, 'clus', split_axis=0, concat_axis=0, tiled=True)  11.5 us
    pallas_call x4, Pallas kernels, call(): pl.pallas_call(kernel, out_shape=outs, in_specs=[spec] * len(operands), o...  5.88 us
  transfers between devices with their start and end apart: 1, of which 1 were waited for; matrix products, arithmetic and copies ran while one was open for 0% of the time, Pallas kernels for 2%

profile of v5, /device:TPU:1, one launch (start us, length us, event | category | flops | bytes accessed | tf_op | source)
XLA Modules:
  0.0 98.8 jit_solution(4554131699389411439)
XLA Ops:
  0.6 0.0 copy-start
  0.6 1.0 copy-done
  1.6 0.0 copy-start.1
  1.6 0.7 copy-done.1
  2.3 0.7 shard_map.41
  3.0 0.2 all_to_all.15
  3.2 48.3 %all_to_all.23 = s16[128,2,896]{2,1,0:T(2,128)(2,1)S(1)} all-to-all(s16[128,2,896]{2,1,0:T(2,128)(2,1)S(1)} %all_to_all.15), channel_id=1, replica_groups=mesh['clus'=128,'src'=4] {'clus'}, dimensions={0} | all-to-all | bytes 917504 | tf_op jit(solution)/shard_map/all_to_all | solution.py:179
  51.5 0.2 all_to_all.17
  51.7 18.0 %all-gather.1.all_ref = s16[1024,896]{1,0:T(8,128)(2,1)S(1)} all-gather(s16[256,896]{1,0:T(8,128)(2,1)S(1)} %all_to_all.17), channel_id=1, replica_groups=mesh['clus'=128,'src'=4] {'src'}, dimensions={0}, use_global_device_ids=true | all-gather | bytes 2293760 | tf_op jit(solution)/shard_map/all_gather | solution.py:190
  69.7 2.1 %shard_map.43 = f32[128,128]{1,0:T(8,128)} custom-call(s16[1024,896]{1,0:T(8,128)(2,1)S(1)} %all-gather.1.all_ref), custom_call_target="tpu_custom_call" | custom-call | tf_op jit(solution)/shard_map/pallas_call | solution.py:168
  71.8 11.5 %all-to-all-start.1 = ((f32[128,1,128]{2,1,0:T(1,128)}), f32[128,1,128]{2,1,0:T(1,128)S(1)}, u32[]{:S(2)}, u32[]{:S(2)}) async-start(f32[128,1,128]{2,1,0:T(1,128)} %bitcast.2), calls=%async_computation.1 | async-start | bytes 131072 | tf_op jit(solution)/shard_map/all_to_all | solution.py:179
  83.3 2.5 %shard_map.42 = f32[8,768]{1,0:T(8,128)} custom-call(s16[1024,896]{1,0:T(8,128)(2,1)S(1)} %all-gather.1.all_ref), custom_call_target="tpu_custom_call" | custom-call | tf_op jit(solution)/shard_map/pallas_call | solution.py:168
  85.8 12.4 %all-to-all-done.1 = f32[128,1,128]{2,1,0:T(1,128)S(1)} async-done(((f32[128,1,128]{2,1,0:T(1,128)}), f32[128,1,128]{2,1,0:T(1,128)S(1)}, u32[]{:S(2)}, u32[]{:S(2)}) %all-to-all-start.1) | async-done | bytes 65568 | tf_op jit(solution)/shard_map/all_to_all | solution.py:179
  98.2 0.6 shard_map.44
Async XLA Ops:
  0.6 1.0 %copy-start = (f32[128,768]{1,0:T(8,128)S(1)}, f32[128,768]{1,0:T(8,128)}, u32[]{:S(2)}) copy-start(f32[128,768]{1,0:T(8,128)} %rows_ref.1) | copy-start | bytes 1179652
  1.6 0.7 copy-start.1
  71.8 26.4 %all-to-all-start.1 = ((f32[128,1,128]{2,1,0:T(1,128)}), f32[128,1,128]{2,1,0:T(1,128)S(1)}, u32[]{:S(2)}, u32[]{:S(2)}) async-start(f32[128,1,128]{2,1,0:T(1,128)} %bitcast.2), calls=%async_computation.1 | async-start | bytes 131072 | tf_op jit(solution)/shard_map/all_to_all | solution.py:179

commit v6 on v5

--- a/solution.py
+++ b/solution.py
@@ -3,9 +3,13 @@
 from jax import lax
 from jax.experimental import pallas as pl
 from jax.experimental.pallas import tpu as pltpu
+from jax.sharding import Mesh
 from jax.sharding import PartitionSpec as P
 
 CLUS_DEV = 8
+AXES = {"z": 16, "x": 4, "core": 2, "yh": 2, "yl": 2}
+OWNER_AXES = ("z", "x", "yh")
+MEET_AXES = ("yl", "core")
 OWNERS = 128
 ROWS = 128
 SLOTS = 256
@@ -123,7 +127,8 @@
             jnp.bfloat16
         )
         member_ref[here, :] = member
-    offset = pl.multiple_of(lax.axis_index("src") * SLOTS, SLOTS)
+    place = lax.axis_index("yl") * 2 + lax.axis_index("core")
+    offset = pl.multiple_of(place * SLOTS, SLOTS)
     own = unit_ref[pl.ds(offset, SLOTS), :]
     own_member = member_ref[pl.ds(offset, SLOTS), :]
     apart = iota((SLOTS, SLOTS), 1) - iota((SLOTS, SLOTS), 0) + offset
@@ -153,6 +158,11 @@
     centroid_ref[...] = sums * lax.rsqrt(jnp.sum(sums * sums, axis=1, keepdims=True) + 1e-06)
 
 
+def choose_kernel(made_ref, other_ref, centroid_ref):
+    mine = lax.axis_index("yh") == lax.axis_index("core")
+    centroid_ref[...] = jnp.where(mine, made_ref[...], other_ref[...])
+
+
 def pick_kernel(returned_ref, code_ref, nearest_ref):
     code = code_ref[...]
     owner = code // 2
@@ -176,7 +186,7 @@
 
 
 def exchange(value):
-    return lax.all_to_all(value, "clus", split_axis=0, concat_axis=0, tiled=True)
+    return lax.all_to_all(value, OWNER_AXES, split_axis=0, concat_axis=0, tiled=True)
 
 
 def on_device(embeddings, cluster):
@@ -187,7 +197,7 @@
         embeddings,
         cluster.reshape(1, ROWS),
     )
-    rows = lax.all_gather(exchange(sent), "src", axis=0, tiled=True)
+    rows = lax.all_gather(exchange(sent), MEET_AXES, axis=0, tiled=True)
     best = call(
         score_kernel,
         shape((OWNERS, 128), jnp.float32),
@@ -198,16 +208,19 @@
         ],
     )
     returned = exchange(best)
-    centroids = call(centroid_kernel, shape((CLUS_DEV, DIM), jnp.float32), rows)
+    made = call(centroid_kernel, shape((CLUS_DEV, DIM), jnp.float32), rows)
+    other = lax.ppermute(made, "yh", [(0, 1), (1, 0)])
+    centroids = call(choose_kernel, shape((CLUS_DEV, DIM), jnp.float32), made, other)
     nearest = call(pick_kernel, shape((1, ROWS), jnp.float32), returned, code)
     return centroids, nearest.reshape(ROWS)
 
 
 def solution(mesh):
+    split = tuple(AXES)
     return jax.shard_map(
         on_device,
-        mesh=mesh,
-        in_specs=(P(("clus", "src"), None), P(("clus", "src"))),
-        out_specs=(P("clus", None), P(("clus", "src"))),
+        mesh=Mesh(mesh.devices.reshape(tuple(AXES.values())), split),
+        in_specs=(P(split, None), P(split)),
+        out_specs=(P(("z", "x", "core"), None), P(split)),
         check_vma=False,
     )

time: 99.1 us -> 97.5 us (0.984)
  waiting for transfers between devices: 12.4 us -> 8.54 us
  starting transfers between devices: 11.5 us -> 13.9 us
    all_to_all x1, waiting for transfers between devices: 12.4 us -> 6.15 us  [exchange(): lax.all_to_all(value, OWNER_AXES, split_axis=0, concat_axis=0, tiled=True)]
    ppermute x0 -> x1, starting transfers between devices: none -> 3.98 us  [on_device(): other = lax.ppermute(made, 'yh', [(0, 1), (1, 0)])]
    ppermute x0 -> x1, waiting for transfers between devices: none -> 2.39 us  [on_device(): other = lax.ppermute(made, 'yh', [(0, 1), (1, 0)])]
    all_to_all x1, starting transfers between devices: 11.5 us -> 9.94 us  [exchange(): lax.all_to_all(value, OWNER_AXES, split_axis=0, concat_axis=0, tiled=True)]
    all_to_all x1, blocking collectives: 48.3 us -> 47.2 us  [exchange(): lax.all_to_all(value, OWNER_AXES, split_axis=0, concat_axis=0, tiled=True)]
    pallas_call x4 -> x5, Pallas kernels: 5.88 us -> 5.88 us  [call(): pl.pallas_call(kernel, out_shape=outs, in_specs=[spec] * len(operands), o...]
  transfers between devices with their start and end apart: 1 -> 2, of which waited for: 1 -> 2; matrix products, arithmetic and copies ran while one was open for 0% -> 0% of each run, Pallas kernels for 2% -> 3%
where the time goes in v6:
time: 97.5 us; the launch traced here: 97.2 us
  blocking collectives  66.1 us (68%)
  starting transfers between devices  13.9 us (14%)
  waiting for transfers between devices  8.54 us (9%)
  Pallas kernels  5.88 us (6%)
  local copies, waits for them, and re-layouts  2.03 us (2%)
    all_to_all x1, blocking collectives, exchange(): lax.all_to_all(value, OWNER_AXES, split_axis=0, concat_axis=0, tiled=True)  47.2 us
    all_gather x1, blocking collectives, on_device(): rows = lax.all_gather(exchange(sent), MEET_AXES, axis=0, tiled=True)  18.9 us
    all_to_all x1, starting transfers between devices, exchange(): lax.all_to_all(value, OWNER_AXES, split_axis=0, concat_axis=0, tiled=True)  9.94 us
    all_to_all x1, waiting for transfers between devices, exchange(): lax.all_to_all(value, OWNER_AXES, split_axis=0, concat_axis=0, tiled=True)  6.15 us
    pallas_call x5, Pallas kernels, call(): pl.pallas_call(kernel, out_shape=outs, in_specs=[spec] * len(operands), o...  5.88 us
    ppermute x1, starting transfers between devices, on_device(): other = lax.ppermute(made, 'yh', [(0, 1), (1, 0)])  3.98 us
    ppermute x1, waiting for transfers between devices, on_device(): other = lax.ppermute(made, 'yh', [(0, 1), (1, 0)])  2.39 us
  transfers between devices with their start and end apart: 2, of which 2 were waited for; matrix products, arithmetic and copies ran while one was open for 0% of the time, Pallas kernels for 3%

profile of v6, /device:TPU:1, one launch (start us, length us, event | category | flops | bytes accessed | tf_op | source)
XLA Modules:
  0.0 97.2 jit_solution(3375743290203568758)
XLA Ops:
  0.6 0.0 copy-start
  0.6 1.0 %copy-done = f32[128,768]{1,0:T(8,128)S(1)} copy-done((f32[128,768]{1,0:T(8,128)S(1)}, f32[128,768]{1,0:T(8,128)}, u32[]{:S(2)}) %copy-start) | copy-done | bytes 393240
  1.6 0.0 copy-start.1
  1.6 0.7 copy-done.1
  2.3 0.7 shard_map.41
  3.0 0.2 all_to_all.15
  3.2 47.2 %all_to_all.23 = s16[128,2,896]{2,1,0:T(2,128)(2,1)S(1)} all-to-all(s16[128,2,896]{2,1,0:T(2,128)(2,1)S(1)} %all_to_all.15), channel_id=1, replica_groups=mesh['z'=16,'x'=4,'core'=2,'yh'=2,'yl'=2] {'z','x','yh'}, dimensions={0} | all-to-all | bytes 917504 | tf_op jit(solution)/shard_map/all_to_all | solution.py:189
  50.3 0.2 all_to_all.17
  50.5 18.9 %all-gather.1.all_ref = s16[1024,896]{1,0:T(8,128)(2,1)S(1)} all-gather(s16[256,896]{1,0:T(8,128)(2,1)S(1)} %all_to_all.17), channel_id=1, replica_groups=mesh['z'=16,'x'=4,'core'=2,'yh'=2,'yl'=2] {'yl','core'}, dimensions={0}, use_global_device_ids=true | all-gather | bytes 2293760 | tf_op jit(solution)/shard_map/all_gather | solution.py:200
  69.5 2.1 %shard_map.44 = f32[128,128]{1,0:T(8,128)} custom-call(s16[1024,896]{1,0:T(8,128)(2,1)S(1)} %all-gather.1.all_ref), custom_call_target="tpu_custom_call" | custom-call | tf_op jit(solution)/shard_map/pallas_call | solution.py:178
  71.6 9.9 %all-to-all-start.1 = ((f32[128,1,128]{2,1,0:T(1,128)}), f32[128,1,128]{2,1,0:T(1,128)S(1)}, u32[]{:S(2)}, u32[]{:S(2)}) async-start(f32[128,1,128]{2,1,0:T(1,128)} %bitcast.2), calls=%async_computation.1 | async-start | bytes 131072 | tf_op jit(solution)/shard_map/all_to_all | solution.py:189
  81.5 1.8 %shard_map.42.made_ref = f32[8,768]{1,0:T(8,128)S(1)} custom-call(s16[1024,896]{1,0:T(8,128)(2,1)S(1)} %all-gather.1.all_ref), custom_call_target="tpu_custom_call" | custom-call | tf_op jit(solution)/shard_map/pallas_call | solution.py:178
  83.4 4.0 %collective-permute-start = (f32[8,768]{1,0:T(8,128)S(1)}, f32[8,768]{1,0:T(8,128)S(1)}, u32[]{:S(2)}, u32[]{:S(2)}) collective-permute-start(f32[8,768]{1,0:T(8,128)S(1)} %shard_map.42.made_ref), channel_id=1, source_target_pairs={{0,2},{2,0},{1,3},{3,1},{4,6},{6,4},{5,7},{7,5},{8,10},{10,8},{9,1... | collective-permute-start | bytes 73736 | tf_op jit(solution)/shard_map/ppermute | solution.py:212
  87.4 2.4 %collective-permute-done.other_ref = f32[8,768]{1,0:T(8,128)S(1)} collective-permute-done((f32[8,768]{1,0:T(8,128)S(1)}, f32[8,768]{1,0:T(8,128)S(1)}, u32[]{:S(2)}, u32[]{:S(2)}) %collective-permute-start) | collective-permute-done | bytes 24608 | tf_op jit(solution)/shard_map/ppermute | solution.py:212
  89.8 0.6 shard_map.43
  90.4 6.2 %all-to-all-done.1 = f32[128,1,128]{2,1,0:T(1,128)S(1)} async-done(((f32[128,1,128]{2,1,0:T(1,128)}), f32[128,1,128]{2,1,0:T(1,128)S(1)}, u32[]{:S(2)}, u32[]{:S(2)}) %all-to-all-start.1) | async-done | bytes 65568 | tf_op jit(solution)/shard_map/all_to_all | solution.py:189
  96.5 0.6 shard_map.45
Async XLA Ops:
  0.6 1.0 %copy-start = (f32[128,768]{1,0:T(8,128)S(1)}, f32[128,768]{1,0:T(8,128)}, u32[]{:S(2)}) copy-start(f32[128,768]{1,0:T(8,128)} %rows_ref.1) | copy-start | bytes 1179652
  1.6 0.7 copy-start.1
  71.6 24.9 %all-to-all-start.1 = ((f32[128,1,128]{2,1,0:T(1,128)}), f32[128,1,128]{2,1,0:T(1,128)S(1)}, u32[]{:S(2)}, u32[]{:S(2)}) async-start(f32[128,1,128]{2,1,0:T(1,128)} %bitcast.2), calls=%async_computation.1 | async-start | bytes 131072 | tf_op jit(solution)/shard_map/all_to_all | solution.py:189
  83.4 6.4 %collective-permute-start = (f32[8,768]{1,0:T(8,128)S(1)}, f32[8,768]{1,0:T(8,128)S(1)}, u32[]{:S(2)}, u32[]{:S(2)}) collective-permute-start(f32[8,768]{1,0:T(8,128)S(1)} %shard_map.42.made_ref), channel_id=1, source_target_pairs={{0,2},{2,0},{1,3},{3,1},{4,6},{6,4},{5,7},{7,5},{8,10},{10,8},{9,1... | collective-permute-start | bytes 73736 | tf_op jit(solution)/shard_map/ppermute | solution.py:212

commit v7 on v6

--- a/solution.py
+++ b/solution.py
@@ -7,9 +7,9 @@
 from jax.sharding import PartitionSpec as P
 
 CLUS_DEV = 8
-AXES = {"z": 16, "x": 4, "core": 2, "yh": 2, "yl": 2}
-OWNER_AXES = ("z", "x", "yh")
-MEET_AXES = ("yl", "core")
+AXES = {"z": 16, "xh": 2, "xl": 2, "core": 2, "y": 4}
+OWNER_AXES = ("z", "xh", "y")
+MEET_AXES = ("xl", "core")
 OWNERS = 128
 ROWS = 128
 SLOTS = 256
@@ -127,7 +127,7 @@
             jnp.bfloat16
         )
         member_ref[here, :] = member
-    place = lax.axis_index("yl") * 2 + lax.axis_index("core")
+    place = lax.axis_index("xl") * 2 + lax.axis_index("core")
     offset = pl.multiple_of(place * SLOTS, SLOTS)
     own = unit_ref[pl.ds(offset, SLOTS), :]
     own_member = member_ref[pl.ds(offset, SLOTS), :]
@@ -158,9 +158,10 @@
     centroid_ref[...] = sums * lax.rsqrt(jnp.sum(sums * sums, axis=1, keepdims=True) + 1e-06)
 
 
-def choose_kernel(made_ref, other_ref, centroid_ref):
-    mine = lax.axis_index("yh") == lax.axis_index("core")
-    centroid_ref[...] = jnp.where(mine, made_ref[...], other_ref[...])
+def choose_kernel(made_ref, centroid_ref):
+    place = lax.axis_index("xl") * 2 + lax.axis_index("core")
+    start = pl.multiple_of(place * CLUS_DEV, CLUS_DEV)
+    centroid_ref[...] = made_ref[pl.ds(start, CLUS_DEV), :]
 
 
 def pick_kernel(returned_ref, code_ref, nearest_ref):
@@ -209,8 +210,8 @@
     )
     returned = exchange(best)
     made = call(centroid_kernel, shape((CLUS_DEV, DIM), jnp.float32), rows)
-    other = lax.ppermute(made, "yh", [(0, 1), (1, 0)])
-    centroids = call(choose_kernel, shape((CLUS_DEV, DIM), jnp.float32), made, other)
+    made = lax.all_gather(made, "y", axis=0, tiled=True)
+    centroids = call(choose_kernel, shape((CLUS_DEV, DIM), jnp.float32), made)
     nearest = call(pick_kernel, shape((1, ROWS), jnp.float32), returned, code)
     return centroids, nearest.reshape(ROWS)
 
@@ -221,6 +222,6 @@
         on_device,
         mesh=Mesh(mesh.devices.reshape(tuple(AXES.values())), split),
         in_specs=(P(split, None), P(split)),
-        out_specs=(P(("z", "x", "core"), None), P(split)),
+        out_specs=(P(("z", "xh", "xl", "core"), None), P(split)),
         check_vma=False,
     )

time: 97.5 us -> 97.5 us (level)
  blocking collectives: 66.1 us -> 77.2 us
  waiting for transfers between devices: 8.54 us -> 2.56 us
  starting transfers between devices: 13.9 us -> 8.9 us
    all_gather x0 -> x1, blocking collectives: none -> 9.95 us  [on_device(): made = lax.all_gather(made, 'y', axis=0, tiled=True)]
    ppermute x1 -> x0, starting transfers between devices: 3.98 us -> none  [on_device(): other = lax.ppermute(made, 'yh', [(0, 1), (1, 0)])]
    all_to_all x1, waiting for transfers between devices: 6.15 us -> 2.56 us  [exchange(): lax.all_to_all(value, OWNER_AXES, split_axis=0, concat_axis=0, tiled=True)]
    ppermute x1 -> x0, waiting for transfers between devices: 2.39 us -> none  [on_device(): other = lax.ppermute(made, 'yh', [(0, 1), (1, 0)])]
    all_to_all x1, blocking collectives: 47.2 us -> 49.1 us  [exchange(): lax.all_to_all(value, OWNER_AXES, split_axis=0, concat_axis=0, tiled=True)]
    all_to_all x1, starting transfers between devices: 9.94 us -> 8.9 us  [exchange(): lax.all_to_all(value, OWNER_AXES, split_axis=0, concat_axis=0, tiled=True)]
  transfers between devices with their start and end apart: 2 -> 1, of which waited for: 2 -> 1; matrix products, arithmetic and copies ran while one was open for 0% -> 0% of each run, Pallas kernels for 3% -> 3%
where the time goes in v7:
time: 97.5 us; the launch traced here: 97.2 us
  blocking collectives  77.2 us (79%)
  starting transfers between devices  8.9 us (9%)
  Pallas kernels  5.88 us (6%)
  waiting for transfers between devices  2.56 us (3%)
  local copies, waits for them, and re-layouts  2.03 us (2%)
    all_to_all x1, blocking collectives, exchange(): lax.all_to_all(value, OWNER_AXES, split_axis=0, concat_axis=0, tiled=True)  49.1 us
    all_gather x1, blocking collectives, on_device(): rows = lax.all_gather(exchange(sent), MEET_AXES, axis=0, tiled=True)  18.2 us
    all_gather x1, blocking collectives, on_device(): made = lax.all_gather(made, 'y', axis=0, tiled=True)  9.95 us
    all_to_all x1, starting transfers between devices, exchange(): lax.all_to_all(value, OWNER_AXES, split_axis=0, concat_axis=0, tiled=True)  8.9 us
    pallas_call x5, Pallas kernels, call(): pl.pallas_call(kernel, out_shape=outs, in_specs=[spec] * len(operands), o...  5.88 us
    all_to_all x1, waiting for transfers between devices, exchange(): lax.all_to_all(value, OWNER_AXES, split_axis=0, concat_axis=0, tiled=True)  2.56 us
  transfers between devices with their start and end apart: 1, of which 1 were waited for; matrix products, arithmetic and copies ran while one was open for 0% of the time, Pallas kernels for 3%

profile of v7, /device:TPU:1, one launch (start us, length us, event | category | flops | bytes accessed | tf_op | source)
XLA Modules:
  0.0 97.2 jit_solution(4634121771328624785)
XLA Ops:
  0.6 0.0 copy-start
  0.6 1.0 %copy-done = f32[128,768]{1,0:T(8,128)S(1)} copy-done((f32[128,768]{1,0:T(8,128)S(1)}, f32[128,768]{1,0:T(8,128)}, u32[]{:S(2)}) %copy-start) | copy-done | bytes 393240
  1.6 0.0 copy-start.1
  1.6 0.7 copy-done.1
  2.3 0.7 shard_map.41
  3.0 0.2 all_to_all.15
  3.2 49.1 %all_to_all.23 = s16[128,2,896]{2,1,0:T(2,128)(2,1)S(1)} all-to-all(s16[128,2,896]{2,1,0:T(2,128)(2,1)S(1)} %all_to_all.15), channel_id=1, replica_groups=mesh['z'=16,'xh'=2,'xl'=2,'core'=2,'y'=4] {'z','xh','y'}, dimensions={0} | all-to-all | bytes 917504 | tf_op jit(solution)/shard_map/all_to_all | solution.py:190
  52.2 0.2 all_to_all.17
  52.4 18.2 %all-gather.1.all_ref = s16[1024,896]{1,0:T(8,128)(2,1)S(1)} all-gather(s16[256,896]{1,0:T(8,128)(2,1)S(1)} %all_to_all.17), channel_id=1, replica_groups=mesh['z'=16,'xh'=2,'xl'=2,'core'=2,'y'=4] {'xl','core'}, dimensions={0}, use_global_device_ids=true | all-gather | bytes 2293760 | tf_op jit(solution)/shard_map/all_gather | solution.py:201
  70.6 2.1 %shard_map.44 = f32[128,128]{1,0:T(8,128)} custom-call(s16[1024,896]{1,0:T(8,128)(2,1)S(1)} %all-gather.1.all_ref), custom_call_target="tpu_custom_call" | custom-call | tf_op jit(solution)/shard_map/pallas_call | solution.py:179
  72.7 8.9 %all-to-all-start.1 = ((f32[128,1,128]{2,1,0:T(1,128)}), f32[128,1,128]{2,1,0:T(1,128)S(1)}, u32[]{:S(2)}, u32[]{:S(2)}) async-start(f32[128,1,128]{2,1,0:T(1,128)} %bitcast.2), calls=%async_computation.1 | async-start | bytes 131072 | tf_op jit(solution)/shard_map/all_to_all | solution.py:190
  81.6 1.8 %shard_map.42 = f32[8,768]{1,0:T(8,128)S(1)} custom-call(s16[1024,896]{1,0:T(8,128)(2,1)S(1)} %all-gather.1.all_ref), custom_call_target="tpu_custom_call" | custom-call | tf_op jit(solution)/shard_map/pallas_call | solution.py:179
  83.5 9.9 %all_gather.7.made_ref = f32[32,768]{1,0:T(8,128)S(1)} all-gather(f32[8,768]{1,0:T(8,128)S(1)} %shard_map.42), channel_id=1, replica_groups=mesh['z'=16,'xh'=2,'xl'=2,'core'=2,'y'=4] {'y'}, dimensions={0}, use_global_device_ids=true | all-gather | bytes 122880 | tf_op jit(solution)/shard_map/all_gather | solution.py:213
  93.4 0.6 shard_map.43
  94.0 2.6 %all-to-all-done.1 = f32[128,1,128]{2,1,0:T(1,128)S(1)} async-done(((f32[128,1,128]{2,1,0:T(1,128)}), f32[128,1,128]{2,1,0:T(1,128)S(1)}, u32[]{:S(2)}, u32[]{:S(2)}) %all-to-all-start.1) | async-done | bytes 65568 | tf_op jit(solution)/shard_map/all_to_all | solution.py:190
  96.6 0.6 shard_map.45
Async XLA Ops:
  0.6 1.0 %copy-start = (f32[128,768]{1,0:T(8,128)S(1)}, f32[128,768]{1,0:T(8,128)}, u32[]{:S(2)}) copy-start(f32[128,768]{1,0:T(8,128)} %rows_ref.1) | copy-start | bytes 1179652
  1.6 0.7 copy-start.1
  72.7 23.9 %all-to-all-start.1 = ((f32[128,1,128]{2,1,0:T(1,128)}), f32[128,1,128]{2,1,0:T(1,128)S(1)}, u32[]{:S(2)}, u32[]{:S(2)}) async-start(f32[128,1,128]{2,1,0:T(1,128)} %bitcast.2), calls=%async_computation.1 | async-start | bytes 131072 | tf_op jit(solution)/shard_map/all_to_all | solution.py:190

commit v8 on v6

--- a/solution.py
+++ b/solution.py
@@ -94,15 +94,18 @@
     fine = jnp.round((factor - coarse * (1.0 / 128.0)) * FINE)
     fields = jnp.where(second == POWER, power, 0.0)
     fields = jnp.where(second == COARSE, coarse, jnp.where(second == COARSE + 1, fine, fields))
+    columns = []
     for group, values in enumerate(groups):
         below = jnp.clip(jnp.floor(top - tops[group]), 0.0, 30.0)
         steps = jnp.round(values * jnp.exp2(15.0 - top + below))
-        here = slice(group * 128, (group + 1) * 128)
-        sent_ref[:, here] = stored(*placed(jnp.clip(steps, -32767.0, 32767.0)))
+        columns.append(jnp.clip(steps, -32767.0, 32767.0))
         fields = jnp.where(second == CLUS_DEV + group, below, fields)
     labels = (first == label).astype(jnp.bfloat16)
-    high, low = placed(fields)
-    sent_ref[:, DIM:] = stored(high, low + product(chosen, labels, ((1,), (1,))))
+    high, low = placed(jnp.concatenate(columns + [fields], axis=1))
+    sent_ref[:, :DIM] = stored(high[:, :DIM], low[:, :DIM])
+    sent_ref[:, DIM:] = stored(
+        high[:, DIM:], low[:, DIM:] + product(chosen, labels, ((1,), (1,)))
+    )
 
 
 def fields_of(ref, here):

time: 97.5 us -> 97.6 us (level)
  no operation moved by 1% of the time
where the time goes in v8:
time: 97.6 us; the launch traced here: 97.3 us
  blocking collectives  66.1 us (68%)
  starting transfers between devices  13.9 us (14%)
  waiting for transfers between devices  8.54 us (9%)
  Pallas kernels  5.98 us (6%)
  local copies, waits for them, and re-layouts  2.03 us (2%)
    all_to_all x1, blocking collectives, exchange(): lax.all_to_all(value, OWNER_AXES, split_axis=0, concat_axis=0, tiled=True)  47.2 us
    all_gather x1, blocking collectives, on_device(): rows = lax.all_gather(exchange(sent), MEET_AXES, axis=0, tiled=True)  18.9 us
    all_to_all x1, starting transfers between devices, exchange(): lax.all_to_all(value, OWNER_AXES, split_axis=0, concat_axis=0, tiled=True)  9.94 us
    all_to_all x1, waiting for transfers between devices, exchange(): lax.all_to_all(value, OWNER_AXES, split_axis=0, concat_axis=0, tiled=True)  6.15 us
    pallas_call x5, Pallas kernels, call(): pl.pallas_call(kernel, out_shape=outs, in_specs=[spec] * len(operands), o...  5.98 us
    ppermute x1, starting transfers between devices, on_device(): other = lax.ppermute(made, 'yh', [(0, 1), (1, 0)])  3.99 us
    ppermute x1, waiting for transfers between devices, on_device(): other = lax.ppermute(made, 'yh', [(0, 1), (1, 0)])  2.39 us
  transfers between devices with their start and end apart: 2, of which 2 were waited for; matrix products, arithmetic and copies ran while one was open for 0% of the time, Pallas kernels for 3%

profile of v8, /device:TPU:1, one launch (start us, length us, event | category | flops | bytes accessed | tf_op | source)
XLA Modules:
  0.0 97.3 jit_solution(1292687691517264151)
XLA Ops:
  0.6 0.0 copy-start
  0.6 1.0 %copy-done = f32[128,768]{1,0:T(8,128)S(1)} copy-done((f32[128,768]{1,0:T(8,128)S(1)}, f32[128,768]{1,0:T(8,128)}, u32[]{:S(2)}) %copy-start) | copy-done | bytes 393240
  1.6 0.0 copy-start.1
  1.6 0.7 copy-done.1
  2.3 0.8 shard_map.41
  3.1 0.2 all_to_all.15
  3.3 47.2 %all_to_all.23 = s16[128,2,896]{2,1,0:T(2,128)(2,1)S(1)} all-to-all(s16[128,2,896]{2,1,0:T(2,128)(2,1)S(1)} %all_to_all.15), channel_id=1, replica_groups=mesh['z'=16,'x'=4,'core'=2,'yh'=2,'yl'=2] {'z','x','yh'}, dimensions={0} | all-to-all | bytes 917504 | tf_op jit(solution)/shard_map/all_to_all | solution.py:192
  50.4 0.2 all_to_all.17
  50.6 18.9 %all-gather.1.all_ref = s16[1024,896]{1,0:T(8,128)(2,1)S(1)} all-gather(s16[256,896]{1,0:T(8,128)(2,1)S(1)} %all_to_all.17), channel_id=1, replica_groups=mesh['z'=16,'x'=4,'core'=2,'yh'=2,'yl'=2] {'yl','core'}, dimensions={0}, use_global_device_ids=true | all-gather | bytes 2293760 | tf_op jit(solution)/shard_map/all_gather | solution.py:203
  69.6 2.1 %shard_map.44 = f32[128,128]{1,0:T(8,128)} custom-call(s16[1024,896]{1,0:T(8,128)(2,1)S(1)} %all-gather.1.all_ref), custom_call_target="tpu_custom_call" | custom-call | tf_op jit(solution)/shard_map/pallas_call | solution.py:181
  71.7 9.9 %all-to-all-start.1 = ((f32[128,1,128]{2,1,0:T(1,128)}), f32[128,1,128]{2,1,0:T(1,128)S(1)}, u32[]{:S(2)}, u32[]{:S(2)}) async-start(f32[128,1,128]{2,1,0:T(1,128)} %bitcast.2), calls=%async_computation.1 | async-start | bytes 131072 | tf_op jit(solution)/shard_map/all_to_all | solution.py:192
  81.6 1.8 %shard_map.42.made_ref = f32[8,768]{1,0:T(8,128)S(1)} custom-call(s16[1024,896]{1,0:T(8,128)(2,1)S(1)} %all-gather.1.all_ref), custom_call_target="tpu_custom_call" | custom-call | tf_op jit(solution)/shard_map/pallas_call | solution.py:181
  83.5 4.0 %collective-permute-start = (f32[8,768]{1,0:T(8,128)S(1)}, f32[8,768]{1,0:T(8,128)S(1)}, u32[]{:S(2)}, u32[]{:S(2)}) collective-permute-start(f32[8,768]{1,0:T(8,128)S(1)} %shard_map.42.made_ref), channel_id=1, source_target_pairs={{0,2},{2,0},{1,3},{3,1},{4,6},{6,4},{5,7},{7,5},{8,10},{10,8},{9,1... | collective-permute-start | bytes 73736 | tf_op jit(solution)/shard_map/ppermute | solution.py:215
  87.5 2.4 %collective-permute-done.other_ref = f32[8,768]{1,0:T(8,128)S(1)} collective-permute-done((f32[8,768]{1,0:T(8,128)S(1)}, f32[8,768]{1,0:T(8,128)S(1)}, u32[]{:S(2)}, u32[]{:S(2)}) %collective-permute-start) | collective-permute-done | bytes 24608 | tf_op jit(solution)/shard_map/ppermute | solution.py:215
  89.9 0.6 shard_map.43
  90.5 6.2 %all-to-all-done.1 = f32[128,1,128]{2,1,0:T(1,128)S(1)} async-done(((f32[128,1,128]{2,1,0:T(1,128)}), f32[128,1,128]{2,1,0:T(1,128)S(1)}, u32[]{:S(2)}, u32[]{:S(2)}) %all-to-all-start.1) | async-done | bytes 65568 | tf_op jit(solution)/shard_map/all_to_all | solution.py:192
  96.6 0.6 shard_map.45
Async XLA Ops:
  0.6 1.0 %copy-start = (f32[128,768]{1,0:T(8,128)S(1)}, f32[128,768]{1,0:T(8,128)}, u32[]{:S(2)}) copy-start(f32[128,768]{1,0:T(8,128)} %rows_ref.1) | copy-start | bytes 1179652
  1.6 0.7 copy-start.1
  71.7 24.9 %all-to-all-start.1 = ((f32[128,1,128]{2,1,0:T(1,128)}), f32[128,1,128]{2,1,0:T(1,128)S(1)}, u32[]{:S(2)}, u32[]{:S(2)}) async-start(f32[128,1,128]{2,1,0:T(1,128)} %bitcast.2), calls=%async_computation.1 | async-start | bytes 131072 | tf_op jit(solution)/shard_map/all_to_all | solution.py:192
  83.5 6.4 %collective-permute-start = (f32[8,768]{1,0:T(8,128)S(1)}, f32[8,768]{1,0:T(8,128)S(1)}, u32[]{:S(2)}, u32[]{:S(2)}) collective-permute-start(f32[8,768]{1,0:T(8,128)S(1)} %shard_map.42.made_ref), channel_id=1, source_target_pairs={{0,2},{2,0},{1,3},{3,1},{4,6},{6,4},{5,7},{7,5},{8,10},{10,8},{9,1... | collective-permute-start | bytes 73736 | tf_op jit(solution)/shard_map/ppermute | solution.py:215

commit v9 on v6

--- a/solution.py
+++ b/solution.py
@@ -16,7 +16,7 @@
 DIM = 768
 WIDE = DIM + 128
 GROUPS = DIM // 128
-HALF = 512
+HALF = 1024
 LEAST_POWER = -2560.0
 COARSE = CLUS_DEV + GROUPS
 POWER = COARSE + 2

time: 97.5 us -> 97.6 us (level)
  no operation moved by 1% of the time
where the time goes in v9:
time: 97.6 us; the launch traced here: 97.3 us
  blocking collectives  66.1 us (68%)
  starting transfers between devices  13.9 us (14%)
  waiting for transfers between devices  8.54 us (9%)
  Pallas kernels  6.01 us (6%)
  local copies, waits for them, and re-layouts  2.03 us (2%)
    all_to_all x1, blocking collectives, exchange(): lax.all_to_all(value, OWNER_AXES, split_axis=0, concat_axis=0, tiled=True)  47.2 us
    all_gather x1, blocking collectives, on_device(): rows = lax.all_gather(exchange(sent), MEET_AXES, axis=0, tiled=True)  18.9 us
    all_to_all x1, starting transfers between devices, exchange(): lax.all_to_all(value, OWNER_AXES, split_axis=0, concat_axis=0, tiled=True)  9.94 us
    all_to_all x1, waiting for transfers between devices, exchange(): lax.all_to_all(value, OWNER_AXES, split_axis=0, concat_axis=0, tiled=True)  6.15 us
    pallas_call x5, Pallas kernels, call(): pl.pallas_call(kernel, out_shape=outs, in_specs=[spec] * len(operands), o...  6.01 us
    ppermute x1, starting transfers between devices, on_device(): other = lax.ppermute(made, 'yh', [(0, 1), (1, 0)])  3.99 us
    ppermute x1, waiting for transfers between devices, on_device(): other = lax.ppermute(made, 'yh', [(0, 1), (1, 0)])  2.39 us
  transfers between devices with their start and end apart: 2, of which 2 were waited for; matrix products, arithmetic and copies ran while one was open for 0% of the time, Pallas kernels for 3%

profile of v9, /device:TPU:1, one launch (start us, length us, event | category | flops | bytes accessed | tf_op | source)
XLA Modules:
  0.0 97.3 jit_solution(895863145219490398)
XLA Ops:
  0.6 0.0 copy-start
  0.6 1.0 %copy-done = f32[128,768]{1,0:T(8,128)S(1)} copy-done((f32[128,768]{1,0:T(8,128)S(1)}, f32[128,768]{1,0:T(8,128)}, u32[]{:S(2)}) %copy-start) | copy-done | bytes 393240
  1.6 0.0 copy-start.1
  1.6 0.7 copy-done.1
  2.3 0.7 shard_map.41
  3.0 0.2 all_to_all.15
  3.2 47.2 %all_to_all.23 = s16[128,2,896]{2,1,0:T(2,128)(2,1)S(1)} all-to-all(s16[128,2,896]{2,1,0:T(2,128)(2,1)S(1)} %all_to_all.15), channel_id=1, replica_groups=mesh['z'=16,'x'=4,'core'=2,'yh'=2,'yl'=2] {'z','x','yh'}, dimensions={0} | all-to-all | bytes 917504 | tf_op jit(solution)/shard_map/all_to_all | solution.py:189
  50.3 0.2 all_to_all.17
  50.5 18.9 %all-gather.1.all_ref = s16[1024,896]{1,0:T(8,128)(2,1)S(1)} all-gather(s16[256,896]{1,0:T(8,128)(2,1)S(1)} %all_to_all.17), channel_id=1, replica_groups=mesh['z'=16,'x'=4,'core'=2,'yh'=2,'yl'=2] {'yl','core'}, dimensions={0}, use_global_device_ids=true | all-gather | bytes 2293760 | tf_op jit(solution)/shard_map/all_gather | solution.py:200
  69.5 2.2 %shard_map.44 = f32[128,128]{1,0:T(8,128)} custom-call(s16[1024,896]{1,0:T(8,128)(2,1)S(1)} %all-gather.1.all_ref), custom_call_target="tpu_custom_call" | custom-call | tf_op jit(solution)/shard_map/pallas_call | solution.py:178
  71.7 9.9 %all-to-all-start.1 = ((f32[128,1,128]{2,1,0:T(1,128)}), f32[128,1,128]{2,1,0:T(1,128)S(1)}, u32[]{:S(2)}, u32[]{:S(2)}) async-start(f32[128,1,128]{2,1,0:T(1,128)} %bitcast.2), calls=%async_computation.1 | async-start | bytes 131072 | tf_op jit(solution)/shard_map/all_to_all | solution.py:189
  81.7 1.8 %shard_map.42.made_ref = f32[8,768]{1,0:T(8,128)S(1)} custom-call(s16[1024,896]{1,0:T(8,128)(2,1)S(1)} %all-gather.1.all_ref), custom_call_target="tpu_custom_call" | custom-call | tf_op jit(solution)/shard_map/pallas_call | solution.py:178
  83.5 4.0 %collective-permute-start = (f32[8,768]{1,0:T(8,128)S(1)}, f32[8,768]{1,0:T(8,128)S(1)}, u32[]{:S(2)}, u32[]{:S(2)}) collective-permute-start(f32[8,768]{1,0:T(8,128)S(1)} %shard_map.42.made_ref), channel_id=1, source_target_pairs={{0,2},{2,0},{1,3},{3,1},{4,6},{6,4},{5,7},{7,5},{8,10},{10,8},{9,1... | collective-permute-start | bytes 73736 | tf_op jit(solution)/shard_map/ppermute | solution.py:212
  87.5 2.4 %collective-permute-done.other_ref = f32[8,768]{1,0:T(8,128)S(1)} collective-permute-done((f32[8,768]{1,0:T(8,128)S(1)}, f32[8,768]{1,0:T(8,128)S(1)}, u32[]{:S(2)}, u32[]{:S(2)}) %collective-permute-start) | collective-permute-done | bytes 24608 | tf_op jit(solution)/shard_map/ppermute | solution.py:212
  89.9 0.6 shard_map.43
  90.5 6.2 %all-to-all-done.1 = f32[128,1,128]{2,1,0:T(1,128)S(1)} async-done(((f32[128,1,128]{2,1,0:T(1,128)}), f32[128,1,128]{2,1,0:T(1,128)S(1)}, u32[]{:S(2)}, u32[]{:S(2)}) %all-to-all-start.1) | async-done | bytes 65568 | tf_op jit(solution)/shard_map/all_to_all | solution.py:189
  96.7 0.6 shard_map.45
Async XLA Ops:
  0.6 1.0 %copy-start = (f32[128,768]{1,0:T(8,128)S(1)}, f32[128,768]{1,0:T(8,128)}, u32[]{:S(2)}) copy-start(f32[128,768]{1,0:T(8,128)} %rows_ref.1) | copy-start | bytes 1179652
  1.6 0.7 copy-start.1
  71.7 24.9 %all-to-all-start.1 = ((f32[128,1,128]{2,1,0:T(1,128)}), f32[128,1,128]{2,1,0:T(1,128)S(1)}, u32[]{:S(2)}, u32[]{:S(2)}) async-start(f32[128,1,128]{2,1,0:T(1,128)} %bitcast.2), calls=%async_computation.1 | async-start | bytes 131072 | tf_op jit(solution)/shard_map/all_to_all | solution.py:189
  83.5 6.4 %collective-permute-start = (f32[8,768]{1,0:T(8,128)S(1)}, f32[8,768]{1,0:T(8,128)S(1)}, u32[]{:S(2)}, u32[]{:S(2)}) collective-permute-start(f32[8,768]{1,0:T(8,128)S(1)} %shard_map.42.made_ref), channel_id=1, source_target_pairs={{0,2},{2,0},{1,3},{3,1},{4,6},{6,4},{5,7},{7,5},{8,10},{10,8},{9,1... | collective-permute-start | bytes 73736 | tf_op jit(solution)/shard_map/ppermute | solution.py:212
